TPU v7x, 32 devices: a whole 2x2x4 slice. The times are simulated.
32 devices in a mesh: fit: 2 (over y), ao: 16 (over z, x, core).
Axes of the slice: x: 2, y: 2, z: 4, core: 2. Of those that a mesh axis runs over, the one named last changes fastest.
Arguments:
- occ_blocks: bfloat16 [6144, 512], P(('fit', 'ao')), may hold values from -6 to 6
- resident: bfloat16 [2048, 4096], P(('fit', 'ao')), may hold values from -0.375 to 0.375
- row_tiles: int32 [32, 2, 24], P(('fit', 'ao')), may hold values from 0 to 23, as said below
- row_pairs: int32 [3, 32, 2, 24], P(None, ('fit', 'ao')), may hold values from -1 to 31, as said below
- live_rows: int32 [32, 2], P(('fit', 'ao')), may hold values from 1 to 24, as said below
- tile_list: int32 [16, 24], replicated, may hold values from 0 to 255, as said below
- owner_slot: int32 [64], replicated, may hold values from 0 to 127, as said below
Outputs:
- half_exchange: bfloat16 [128, 64, 512], P('ao', 'fit')
Inputs may be any that keep to these rules, and one draw needn't show every extreme that they name: `row_tiles`: within each group and cycle step the 24 entries are a permutation of 0 to 23. `row_pairs`: each entry is a resident tile index, or -1 where the row has no tile for that fitting block; rows at or beyond live_rows are -1. Within a group and cycle step, live rows whose tiles share an AO block name the same resident tile for the same fitting block. `live_rows`: in every draw some group has all 24 rows live at some cycle step. `tile_list`: codes within a column are distinct and name AO blocks that some owner holds. A column names at most 2 tiles whose AO blocks belong to one owner device (owner_slot // 8); in every draw some owner gets exactly 2 from every column. AO blocks take distinct slots; the owner device of block b is owner_slot[b] // 8; an owner holds 0 to 8 blocks in its first slots, and some owner holds exactly 8.
All inputs are finite; a program needn't handle non-finite values.
Results may differ from a plain program's by a relative error of at most 0.001.
Values may be sent and summed in bfloat16 or wider, within the bound.
No kernel may reach another device: no remote copies, remote signals or barrier semaphores. Data moves between devices by JAX's collectives and lax.ppermute only.
A program may use at most 64 MiB of HBM per device.

v0:
```python
import jax
import jax.numpy as jnp
from jax import lax
from jax.sharding import PartitionSpec as P

AB = 64
FB = 64
OB = 128
OWN_CAP = 8
CAP = 2


def from_behind(block, axis, distance):
    devices = range(lax.axis_size(axis))
    route = [((i - distance) % len(devices), i) for i in devices]
    return lax.ppermute(block, axis, route)


def contract(
    partial_value, upiece, cycle_step, resident, row_tiles, row_pairs, live_rows, tile_occ
):
    fit_count = live_rows.shape[1]
    pair_step = resident.shape[0] // fit_count
    row_width = row_tiles.shape[2]
    block_rows = row_width // 3
    fit_blocks = row_pairs.shape[0]
    occ_count = upiece.shape[1] // OB
    grouped = upiece.reshape(fit_blocks, FB, occ_count, OB)
    step_tiles = lax.dynamic_index_in_dim(row_tiles[0], cycle_step, 0, keepdims=False)
    step_pairs = lax.dynamic_index_in_dim(row_pairs[:, 0], cycle_step, 1, keepdims=False)
    live_count = lax.dynamic_index_in_dim(live_rows[0], cycle_step, 0, keepdims=False)

    def one_block(block_num, running):
        offset = block_num * block_rows
        tile_ids = lax.dynamic_slice_in_dim(step_tiles, offset, block_rows)
        pair_ids = lax.dynamic_slice_in_dim(step_pairs, offset, block_rows, axis=1)
        in_range = offset + jnp.arange(block_rows) < live_count
        usable = (pair_ids >= 0) & in_range[None, :]
        picked = resident[cycle_step * pair_step + jnp.maximum(pair_ids, 0)]
        picked = jnp.where(usable[:, :, None], picked, jnp.zeros((), picked.dtype))
        picked = picked.reshape(fit_blocks, block_rows, AB, FB)
        chosen = grouped[:, :, tile_occ[tile_ids], :]
        product = jnp.einsum("jrmp,jprc->rmc", picked, chosen, preferred_element_type=jnp.float32)
        return running.at[tile_ids].add(product)

    block_total = (live_count + block_rows - 1) // block_rows
    return lax.fori_loop(0, block_total, one_block, partial_value)


def routing(tile_list, owner_slot, occ_count):
    row_width = tile_list.shape[1]
    slot_ids = owner_slot[tile_list // occ_count]
    owners = slot_ids // OWN_CAP
    same_owner = owners[:, :, None] == owners[:, None, :]
    earlier = jnp.arange(row_width)[None, :] < jnp.arange(row_width)[:, None]
    owner_ranks = jnp.sum((same_owner & earlier[None, :, :]).astype(jnp.int32), axis=2)
    targets = slot_ids % OWN_CAP * occ_count + tile_list % occ_count
    return (owners, owner_ranks, targets)


def pack_tiles(tiles_here, owners_row, ranks_row, ao_count):
    buffer = jnp.zeros((ao_count * CAP,) + tiles_here.shape[1:], tiles_here.dtype)
    buffer = buffer.at[owners_row * CAP + ranks_row].set(tiles_here)
    return buffer.reshape((ao_count, CAP) + tiles_here.shape[1:])


def unpack(received, owners, owner_ranks, targets, column, occ_count):
    ao_count = owners.shape[0]
    received = received.reshape((ao_count * CAP,) + received.shape[2:])
    position = jnp.arange(ao_count)[:, None] * CAP + owner_ranks
    position = jnp.where(owners == column, position, ao_count * CAP)
    target_at = jnp.full((ao_count * CAP,), OWN_CAP * occ_count, jnp.int32)
    target_at = target_at.at[position.reshape(-1)].set(targets.reshape(-1), mode="drop")
    summed = jnp.zeros((OWN_CAP * occ_count,) + received.shape[1:], jnp.float32)
    summed = summed.at[target_at].add(received, mode="drop")
    height = received.shape[1]
    return (
        summed.reshape(OWN_CAP, occ_count, height, OB)
        .transpose(0, 2, 1, 3)
        .reshape(OWN_CAP, height, occ_count * OB)
    )


def shards(occ_blocks, resident, row_tiles, row_pairs, live_rows, tile_list, owner_slot):
    fit_count = lax.axis_size("fit")
    ao_count = lax.axis_size("ao")
    column = lax.axis_index("ao")
    occ_count = occ_blocks.shape[1] // OB
    tile_codes = lax.dynamic_index_in_dim(tile_list, column, 0, keepdims=False)
    tile_occ = tile_codes % occ_count
    row_width = tile_list.shape[1]
    partial_value = jnp.zeros((row_width, AB, OB), jnp.float32)

    def advance(running, upiece, cycle_step):
        return contract(
            running, upiece, cycle_step, resident, row_tiles, row_pairs, live_rows, tile_occ
        )

    partial_value = advance(partial_value, occ_blocks, 0)

    def cycle_turn(cycle_step, cycle_state):
        upiece, running = cycle_state
        upiece = from_behind(upiece, "fit", 1)
        return (upiece, advance(running, upiece, cycle_step))

    _, partial_value = lax.fori_loop(1, fit_count, cycle_turn, (occ_blocks, partial_value))
    owners, owner_ranks, targets = routing(tile_list, owner_slot, occ_count)
    owners_row = lax.dynamic_index_in_dim(owners, column, 0, keepdims=False)
    ranks_row = lax.dynamic_index_in_dim(owner_ranks, column, 0, keepdims=False)
    outgoing = pack_tiles(partial_value, owners_row, ranks_row, ao_count)
    received = lax.all_to_all(outgoing, "ao", split_axis=0, concat_axis=0, tiled=True)
    summed = unpack(received, owners, owner_ranks, targets, column, occ_count)
    result = lax.psum_scatter(summed, "fit", scatter_dimension=1, tiled=True)
    return result.astype(jnp.bfloat16)


def solution(mesh):
    return jax.shard_map(
        shards,
        mesh=mesh,
        in_specs=(
            P(("fit", "ao"), None),
            P(("fit", "ao"), None),
            P(("fit", "ao"), None, None),
            P(None, ("fit", "ao"), None, None),
            P(("fit", "ao"), None),
            P(),
            P(),
        ),
        out_specs=P("ao", "fit", None),
        check_vma=False,
    )
```

profile of v0, /device:TPU:0, one launch (start us, length us, event | category | flops | bytes accessed | tf_op | source)
XLA Modules:
  0.0 115.6 jit_solution(464199938242058591)
XLA Ops:
  6.5 3.0 %collective-permute-start = (bf16[192,512]{1,0:T(8,128)(2,1)}, bf16[192,512]{1,0:T(8,128)(2,1)S(1)}, u32[]{:S(2)}, u32[]{:S(2)}) collective-permute-start(bf16[192,512]{1,0:T(8,128)(2,1)} %param.11), channel_id=1, source_target_pairs={{16,0},{0,16},{17,1},{1,17},{18,2},{2,18},{19,3},{3,19},{20,4},{4,... | collective-permute-start | bytes 589832 | tf_op jit(solution)/shard_map/while/body/eval_jaxpr/ppermute | solution.py:16
  9.5 0.7 copy-done.4
  10.2 0.7 fusion.25
  12.1 1.0 reshape.277
  13.2 0.6 copy-done.5
  13.8 0.7 copy-done.3
  14.5 0.1 reshape.333
  14.6 2.7 %gather_fusion.6 = s32[384]{0:T(512)S(1)} fusion(s32[64]{0:T(128)S(1)} %copy-done, s32[1024]{0:T(1024)S(1)} %pad_clamp_fusion.6), kind=kCustom, calls=%fused_computation.6 | custom fusion | bytes 4608 | tf_op jit(solution)/shard_map/gather | solution.py:52
  17.3 0.1 reshape.332
  17.6 0.9 copy-done.1
  18.5 9.3 %while.32 = (s32[]{:T(128)}, f32[24,64,128]{2,1,0:T(8,128)S(1)}, s32[]{:T(128)}, s32[24]{0:T(128)S(1)}, s32[3,24]{1,0:T(4,128)S(1)}, /*index=5*/s32[]{:T(128)}, ...) while((s32[]{:T(128)}, f32[24,64,128]{2,1,0:T(8,128)S(1)}, ...), condition=%wide.region_4.5_spmd, body=%wide.region_2.4_spmd.sunk | while | flops 25332876 | bytes 3224879 | solution.py:47
  18.5 0.6 add_compare_fusion.4
  19.1 0.1 compare_and_fusion.4
  19.2 0.1 copy.52
  19.4 0.1 reshape.424
  19.5 0.6 gather_fusion
  20.1 0.7 gather_fusion.2
  20.8 0.4 gather.74
  21.2 0.6 gather_fusion.1
  21.8 0.4 convolution_bitcast_fusion.4
  22.2 0.9 scatter_fusion
  23.1 0.6 add_compare_fusion.4
  23.7 0.1 compare_and_fusion.4
  23.9 0.1 copy.52
  24.0 0.1 reshape.424
  24.1 0.6 gather_fusion
  24.8 0.7 gather_fusion.2
  25.5 0.4 gather.74
  25.9 0.6 gather_fusion.1
  26.5 0.4 convolution_bitcast_fusion.4
  26.9 0.9 scatter_fusion
  27.8 0.4 convert_reduce_fusion
  28.4 9.6 %while.33 = (s32[]{:T(128)}, f32[24,64,128]{2,1,0:T(8,128)S(1)}, s32[]{:T(128)}, s32[24]{0:T(128)S(1)}, s32[3,24]{1,0:T(4,128)S(1)}, /*index=5*/s32[]{:T(128)}, ...) while((s32[]{:T(128)}, f32[24,64,128]{2,1,0:T(8,128)S(1)}, ...), condition=%wide.region_7.8_spmd, body=%wide.region_5.7_spmd.sunk | while | flops 25332972 | bytes 3224879 | solution.py:47
  28.4 0.7 add_compare_fusion.5
  29.1 0.1 compare_and_fusion.5
  29.2 0.1 copy.54
  29.4 0.1 reshape.433
  29.5 0.6 gather_fusion.3
  30.2 0.7 gather_fusion.5
  30.9 0.4 gather.78
  31.2 0.6 gather_fusion.4
  31.9 0.4 convolution_bitcast_fusion.5
  32.3 0.9 scatter_fusion.1
  33.2 0.7 add_compare_fusion.5
  34.0 0.1 copy.54
  34.2 0.1 reshape.433
  34.3 0.6 gather_fusion.3
  35.0 0.7 gather_fusion.5
  35.6 0.4 gather.78
  36.0 0.6 gather_fusion.4
  36.6 0.4 convolution_bitcast_fusion.5
  37.0 0.9 scatter_fusion.1
  37.9 1.1 broadcast.348.clone
  39.1 4.5 %scatter_fusion.2 = f32[32,64,128]{2,1,0:T(8,128)} fusion(f32[32,64,128]{2,1,0:T(8,128)} %broadcast.348.clone, s32[24]{0:T(128)S(1)} %fusion.21, f32[24,64,128]{2,1,0:T(8,128)S(1)} %get-tuple-element.230), kind=kCustom, calls=%fused_computation.10 | custom fusion | bytes 2359392 | tf_op jit(solution)/shard_map/scatter | solution.py:63
  43.6 15.4 %all-to-all-start = ((f32[16,2,64,128]{3,2,1,0:T(8,128)}), f32[16,2,64,128]{3,2,1,0:T(8,128)S(1)}, u32[]{:S(2)}, u32[]{:S(2)}) async-start(f32[16,2,64,128]{3,2,1,0:T(8,128)} %bitcast.17), calls=%async_computation | async-start | bytes 2097152 | tf_op jit(solution)/shard_map/all_to_all | solution.py:111
  59.0 0.1 reshape.359
  59.2 0.1 add.254
  59.3 2.9 %scatter_custom_fusion.2 = s32[32]{0:T(128)S(1)} fusion(s32[384]{0:T(512)S(1)} %fusion.16, s32[384]{0:T(512)S(1)} %reshape.359, s32[]{:T(128)} %constant.206.clone.1), kind=kCustom, calls=%fused_computation.91 | custom fusion | bytes 132 | tf_op jit(solution)/shard_map/scatter | solution.py:73
  62.2 19.7 %all-to-all-done = f32[16,2,64,128]{3,2,1,0:T(8,128)S(1)} async-done(((f32[16,2,64,128]{3,2,1,0:T(8,128)}), f32[16,2,64,128]{3,2,1,0:T(8,128)S(1)}, u32[]{:S(2)}, u32[]{:S(2)}) %all-to-all-start) | async-done | bytes 1048608 | tf_op jit(solution)/shard_map/all_to_all | solution.py:111
  81.9 0.1 broadcast.348
  82.0 2.1 %scatter_fusion.3 = f32[32,64,128]{2,1,0:T(8,128)S(1)} fusion(f32[32,64,128]{2,1,0:T(8,128)S(1)} %broadcast.348, s32[32]{0:T(128)S(1)} %compare_select_fusion.12, f32[32,64,128]{2,1,0:T(8,128)S(1)} %bitcast.70), kind=kCustom, calls=%fused_computation.11 | custom fusion | flops 262144 | bytes 3145856 | tf_op jit(solution)/shard_map/scatter-add | solution.py:75
  84.2 1.1 copy.44
  85.3 21.7 %reduce-scatter.2.cloned.1.call-done = f32[8,32,512]{2,1,0:T(8,128)} async-done(((f32[8,64,512]{2,1,0:T(8,128)}), f32[8,32,512]{2,1,0:T(8,128)}) %reduce-scatter.2.cloned.1.call-update) | async-done | bytes 524304 | tf_op jit(solution)/shard_map/reduce_scatter | solution.py:113
  107.0 1.8 %convert_element_type.7 = bf16[8,32,512]{2,1,0:T(8,128)(2,1)} convert(f32[8,32,512]{2,1,0:T(8,128)} %reduce-scatter.2.cloned.1.call-done) | non-fusion elementwise | flops 131072 | bytes 786432 | tf_op jit(solution)/shard_map/convert_element_type | solution.py:114
  (54 shorter events, 1.3 us)
Async XLA Ops:
  6.5 8.1 %copy-start = (s32[64]{0:T(128)S(1)}, s32[64]{0:T(128)}, u32[]{:S(2)}) copy-start(s32[64]{0:T(128)} %param.17) | copy-start | bytes 772
  6.5 21.7 %collective-permute-start = (bf16[192,512]{1,0:T(8,128)(2,1)}, bf16[192,512]{1,0:T(8,128)(2,1)S(1)}, u32[]{:S(2)}, u32[]{:S(2)}) collective-permute-start(bf16[192,512]{1,0:T(8,128)(2,1)} %param.11), channel_id=1, source_target_pairs={{16,0},{0,16},{17,1},{1,17},{18,2},{2,18},{19,3},{3,19},{20,4},{4,... | collective-permute-start | bytes 589832 | tf_op jit(solution)/shard_map/while/body/eval_jaxpr/ppermute | solution.py:16
  9.5 0.7 copy-start.4
  12.1 1.0 copy-start.2
  13.1 0.7 copy-start.5
  13.8 0.7 copy-start.3
  17.4 1.0 copy-start.1
  43.6 38.3 %all-to-all-start = ((f32[16,2,64,128]{3,2,1,0:T(8,128)}), f32[16,2,64,128]{3,2,1,0:T(8,128)S(1)}, u32[]{:S(2)}, u32[]{:S(2)}) async-start(f32[16,2,64,128]{3,2,1,0:T(8,128)} %bitcast.17), calls=%async_computation | async-start | bytes 2097152 | tf_op jit(solution)/shard_map/all_to_all | solution.py:111
  59.0 48.1 %reduce-scatter.2.cloned.1.call-start = ((), (), s32[]{:S(2)}) async-start(), calls=%async_computation.2 | async-start | bytes 1572864 | tf_op jit(solution)/shard_map/reduce_scatter | solution.py:113
Sparse Core Ops, SparseCore 0:
  85.4 21.5 reduce-scatter.1
where the time goes:
time: 116 us
  waiting for transfers between devices  41.4 us (36%)
  local copies, waits for them, and re-layouts  27.5 us (24%)
  starting transfers between devices  18.4 us (16%)
  between operations  14.9 us (13%)
  other arithmetic  11.6 us (10%)
  matrix products  1.52 us (1%)
    reduce_scatter x1, waiting for transfers between devices, shards(): result = lax.psum_scatter(summed, 'fit', scatter_dimension=1, tiled=True)  21.7 us
    all_to_all x1, waiting for transfers between devices, shards(): lax.all_to_all(outgoing, 'ao', split_axis=0, concat_axis=0, tiled=True)  19.7 us
    all_to_all x1, starting transfers between devices, shards(): lax.all_to_all(outgoing, 'ao', split_axis=0, concat_axis=0, tiled=True)  15.4 us
    gather x8, local copies, waits for them, and re-layouts, one_block(): chosen = grouped[:, :, tile_occ[tile_ids], :]  5.09 us
    scatter x1, local copies, waits for them, and re-layouts, pack_tiles(): buffer = buffer.at[owners_row * CAP + ranks_row].set(tiles_here)  4.54 us
    gather x8, local copies, waits for them, and re-layouts, one_block(): picked = resident[cycle_step * pair_step + jnp.maximum(pair_ids, 0)]  4.13 us
    scatter-add x4, other arithmetic, one_block(): return running.at[tile_ids].add(product)  3.55 us
    ppermute x1, starting transfers between devices, from_behind(): return lax.ppermute(block, axis, route)  2.97 us
  transfers between devices with their start and end apart: 3, of which 2 were waited for; matrix products, arithmetic and copies ran while one was open for 15% of the time, Pallas kernels for 0%

commit v1 on v0

v1 whole, which is shorter than its diff:
```python
import functools

import jax
import jax.numpy as jnp
from jax import lax
from jax.experimental import pallas as pl
from jax.experimental.pallas import tpu as pltpu
from jax.sharding import PartitionSpec as P

AB = 64
FB = 64
OB = 128
OWN_CAP = 8
CAP = 2
LEVELS = 32700.0
LOWEST = -100.0
BIAS = 127.0
NEAREST = 12582912.0
LIMIT = 48 * 1024 * 1024

SMEM = pl.BlockSpec(memory_space=pltpu.SMEM)
VMEM = pl.BlockSpec(memory_space=pltpu.VMEM)


def from_behind(block, axis, distance):
    count = lax.axis_size(axis)
    return lax.ppermute(block, axis, [((i - distance) % count, i) for i in range(count)])


def rounded(value):
    return (value + NEAREST) - NEAREST


def occ_columns(ref, occ_block):
    return ref[:, pl.ds(pl.multiple_of(occ_block * OB, OB), OB)]


def first_step(
    column_ref, rows_ref, pairs_ref, live_ref, list_ref, slot_ref, list_vec, tiles_ref, occ_ref,
    total_ref, later_ref, occ_of_ref, target_ref,
    sid_of_tile, held, pair_of,
):
    steps, width = rows_ref.shape[1:]
    fit_blocks = pairs_ref.shape[0]
    ao_count = list_ref.shape[0]
    slots = ao_count * CAP
    pair_step = tiles_ref.shape[0] // steps
    occ_count = occ_ref.shape[1] // OB
    column = column_ref[0]

    def clear_owner(owner, _):
        held[owner] = 0
        return 0

    def clear_slot(slot, _):
        occ_of_ref[slot] = 0
        for at in range(steps * fit_blocks):
            pair_of[at * slots + slot] = -1
        return 0

    lax.fori_loop(0, ao_count, clear_owner, 0, unroll=8)
    lax.fori_loop(0, slots, clear_slot, 0, unroll=8)

    def route(tile, _):
        code = list_ref[column, tile]
        owner = lax.div(slot_ref[lax.div(code, occ_count)], OWN_CAP)
        rank = held[owner]
        held[owner] = rank + 1
        slot = owner * CAP + rank
        sid_of_tile[tile] = slot
        occ_of_ref[slot] = lax.rem(code, occ_count)
        return 0

    lax.fori_loop(0, width, route, 0, unroll=4)

    for step in range(steps):
        live = live_ref[0, step]

        def place(row, _):
            slot = sid_of_tile[rows_ref[0, step, row]]
            for j in range(fit_blocks):
                pair = pairs_ref[j, 0, step, row]
                usable = (pair >= 0) & (row < live)
                pair_of[(step * fit_blocks + j) * slots + slot] = jnp.where(
                    usable, pair + step * pair_step, -1
                )
            return 0

        lax.fori_loop(0, width, place, 0, unroll=4)

    def tile_at(step, j, slot):
        pair = pair_of[(step * fit_blocks + j) * slots + slot]
        picked = tiles_ref[jnp.maximum(pair, 0)]
        return jnp.where(pair >= 0, picked, jnp.zeros_like(picked))

    def one_slot(slot, _):
        for step in range(steps):
            left = jnp.concatenate([tile_at(step, j, slot) for j in range(fit_blocks)], axis=1)
            if step:
                later_ref[step - 1, slot] = left
            else:
                total_ref[slot] = jnp.dot(
                    left, occ_columns(occ_ref, occ_of_ref[slot]), preferred_element_type=jnp.float32
                )
        return 0

    lax.fori_loop(0, slots, one_slot, 0, unroll=8)

    codes = list_vec[...]
    blocks = codes // occ_count
    slot_ids = jnp.zeros_like(codes)
    for block in range(slot_ref.shape[0]):
        slot_ids = jnp.where(blocks == block, slot_ref[block], slot_ids)
    mine = slot_ids // OWN_CAP == column
    count = OWN_CAP * occ_count
    goal = slot_ids % OWN_CAP * occ_count + codes % occ_count
    key = lax.broadcasted_iota(jnp.int32, codes.shape, 1) * count + goal
    first = jnp.min(jnp.where(mine, key, width * count), axis=1, keepdims=True)
    last = jnp.max(jnp.where(mine, key, -1), axis=1, keepdims=True)
    first_goal = jnp.where(last >= 0, first % count, count)
    last_goal = jnp.where(last > first, last % count, count)
    lane = lax.broadcasted_iota(jnp.int32, target_ref.shape, 1)
    target_ref[...] = jnp.where(lane == 0, first_goal, last_goal)


def middle_step(occ_of_ref, later_ref, occ_ref, before_ref, total_ref):
    def one_slot(slot, _):
        total_ref[slot] = before_ref[slot] + jnp.dot(
            later_ref[slot], occ_columns(occ_ref, occ_of_ref[slot]), preferred_element_type=jnp.float32
        )
        return 0

    lax.fori_loop(0, total_ref.shape[0], one_slot, 0, unroll=4)


def coded(value):
    top = jnp.max(jnp.abs(value), axis=0, keepdims=True)
    power = jnp.ceil(jnp.log2(jnp.maximum(top, 2.0**LOWEST)))
    scaled = value * (LEVELS * jnp.exp2(-power))
    bits = (power + BIAS).astype(jnp.int32)
    sub = lax.broadcasted_iota(jnp.int32, (8, OB), 0)
    bit = lax.shift_right_logical(jnp.broadcast_to(bits, (8, OB)), sub) & 1
    head = scaled[:8]
    bit_value = bit.astype(jnp.float32)
    head = rounded((head - bit_value) * 0.5) * 2.0 + bit_value
    if value.shape[0] == 8:
        return head.astype(jnp.int32)
    return jnp.concatenate([head, rounded(scaled[8:])], axis=0).astype(jnp.int32)


def decoded(whole):
    sub = lax.broadcasted_iota(jnp.int32, (8, OB), 0)
    bits = jnp.sum(lax.shift_left(whole[:8] & 1, sub), axis=0, keepdims=True)
    scale = jnp.exp2(bits.astype(jnp.float32) - BIAS) * (1.0 / LEVELS)
    return whole.astype(jnp.float32) * scale


def last_step(occ_of_ref, later_ref, occ_ref, before_ref, out_ref):
    height = out_ref.shape[1]
    fit_count = AB // height
    ao_count = out_ref.shape[0] // fit_count

    def one_owner(owner, _):
        sums = []
        for rank in range(CAP):
            slot = owner * CAP + rank
            sums.append(
                before_ref[slot]
                + jnp.dot(
                    later_ref[slot],
                    occ_columns(occ_ref, occ_of_ref[slot]),
                    preferred_element_type=jnp.float32,
                )
            )
        for part in range(fit_count):
            low, high = [coded(total[part * height : (part + 1) * height]) for total in sums]
            out_ref[part * ao_count + owner] = (low & 0xFFFF) | lax.shift_left(high, 16)
        return 0

    lax.fori_loop(0, ao_count, one_owner, 0, unroll=4)


def collect(target_ref, received_ref, out_ref, sums):
    ao_count = target_ref.shape[0]
    occ_count = out_ref.shape[2] // OB
    sums[...] = jnp.zeros_like(sums)

    def one_source(source, _):
        column = lax.rem(source, ao_count)
        words = received_ref[source]
        low = lax.shift_right_arithmetic(lax.shift_left(words, 16), 16)
        high = lax.shift_right_arithmetic(words, 16)
        first, second = target_ref[column, 0], target_ref[column, 1]
        sums[first] += decoded(low)
        sums[second] += decoded(high)
        return 0

    lax.fori_loop(0, received_ref.shape[0], one_source, 0, unroll=8)
    for slot in range(OWN_CAP):
        for occ in range(occ_count):
            out_ref[slot, :, occ * OB : (occ + 1) * OB] = sums[slot * occ_count + occ].astype(
                out_ref.dtype
            )


def shards(occ_blocks, resident, row_tiles, row_pairs, live_rows, tile_list, owner_slot):
    fit_count = lax.axis_size("fit")
    ao_count = lax.axis_size("ao")
    fit_blocks = row_pairs.shape[0]
    depth = fit_blocks * FB
    width = tile_list.shape[1]
    slots = ao_count * CAP
    height = AB // fit_count
    occ_count = occ_blocks.shape[1] // OB
    column = lax.axis_index("ao").astype(jnp.int32).reshape(1)
    params = pltpu.CompilerParams(vmem_limit_bytes=LIMIT)

    incoming = from_behind(occ_blocks, "fit", 1)
    tiles = resident.reshape(resident.shape[0], AB, FB)
    total_shape = jax.ShapeDtypeStruct((slots, AB, OB), jnp.float32)
    total, later, occ_of, targets = pl.pallas_call(
        first_step,
        out_shape=(
            total_shape,
            jax.ShapeDtypeStruct((fit_count - 1, slots, AB, depth), jnp.bfloat16),
            jax.ShapeDtypeStruct((slots,), jnp.int32),
            jax.ShapeDtypeStruct((ao_count, OB), jnp.int32),
        ),
        in_specs=[SMEM] * 6 + [VMEM] * 3,
        out_specs=(VMEM, VMEM, SMEM, VMEM),
        scratch_shapes=[
            pltpu.SMEM((width,), jnp.int32),
            pltpu.SMEM((ao_count,), jnp.int32),
            pltpu.SMEM((fit_count * fit_blocks * slots,), jnp.int32),
        ],
        compiler_params=params,
    )(column, row_tiles, row_pairs, live_rows, tile_list, owner_slot, tile_list, tiles, occ_blocks)

    def step_specs(step):
        at_step = pl.BlockSpec((None, slots, AB, depth), lambda at: (step - 1, 0, 0, 0))
        return dict(grid=(1,), in_specs=[SMEM, at_step, VMEM, VMEM], out_specs=VMEM)

    for step in range(1, fit_count - 1):
        total = pl.pallas_call(
            middle_step, out_shape=total_shape, compiler_params=params, **step_specs(step)
        )(occ_of, later, incoming, total)
        incoming = from_behind(incoming, "fit", 1)

    outgoing = pl.pallas_call(
        last_step,
        out_shape=jax.ShapeDtypeStruct((fit_count * ao_count, height, OB), jnp.int32),
        compiler_params=params,
        **step_specs(fit_count - 1),
    )(occ_of, later, incoming, total)
    received = lax.all_to_all(outgoing, ("fit", "ao"), split_axis=0, concat_axis=0, tiled=True)
    return pl.pallas_call(
        collect,
        out_shape=jax.ShapeDtypeStruct((OWN_CAP, height, occ_count * OB), jnp.bfloat16),
        in_specs=[SMEM, VMEM],
        out_specs=VMEM,
        scratch_shapes=[pltpu.VMEM((OWN_CAP * occ_count + 1, height, OB), jnp.float32)],
        compiler_params=params,
    )(targets, received)


def solution(mesh):
    return jax.shard_map(
        shards,
        mesh=mesh,
        in_specs=(
            P(("fit", "ao"), None),
            P(("fit", "ao"), None),
            P(("fit", "ao"), None, None),
            P(None, ("fit", "ao"), None, None),
            P(("fit", "ao"), None),
            P(),
            P(),
        ),
        out_specs=P("ao", "fit", None),
        check_vma=False,
    )
```

time: 116 us -> 33.8 us (0.29)
  waiting for transfers between devices: 41.4 us -> 0.01 us
  local copies, waits for them, and re-layouts: 27.5 us -> 2.74 us
  blocking collectives: 0 us -> 20.6 us
  starting transfers between devices: 18.4 us -> 2.97 us
  between operations: 14.9 us -> 0.09 us
  other arithmetic: 11.6 us -> 0 us
  Pallas kernels: 0 us -> 7.15 us
  matrix products: 1.52 us -> 0 us
    reduce_scatter x1 -> x0, waiting for transfers between devices: 21.7 us -> none  [shards(): result = lax.psum_scatter(summed, 'fit', scatter_dimension=1, tiled=True)]
    all_to_all x0 -> x1, blocking collectives: none -> 20.6 us  [shards(): lax.all_to_all(outgoing, ('fit', 'ao'), split_axis=0, concat_axis=0, tile...]
    all_to_all x1 -> x0, waiting for transfers between devices: 19.7 us -> none  [shards(): lax.all_to_all(outgoing, 'ao', split_axis=0, concat_axis=0, tiled=True)]
    all_to_all x1 -> x0, starting transfers between devices: 15.4 us -> none  [shards(): lax.all_to_all(outgoing, 'ao', split_axis=0, concat_axis=0, tiled=True)]
    gather x18 -> x0, local copies, waits for them, and re-layouts: 12 us -> none  [the longest x8 5.09 us: one_block(): chosen = grouped[:, :, tile_occ[tile_ids], :]]
    scatter x2 -> x0, local copies, waits for them, and re-layouts: 7.46 us -> none  [the longest x1 4.54 us: pack_tiles(): buffer = buffer.at[owners_row * CAP + ranks_row].set(tiles_here)]
    pallas_call x0 -> x3, Pallas kernels: none -> 7.15 us  [the longest x1 3.46 us: shards(): pl.pallas_call(first_step, out_shape=(total_shape, jax.ShapeDtypeStruct((...]
    scatter-add x5 -> x0, other arithmetic: 5.69 us -> none  [the longest x4 3.55 us: one_block(): return running.at[tile_ids].add(product)]
  transfers between devices with their start and end apart: 3 -> 1, of which waited for: 2 -> 0; matrix products, arithmetic and copies ran while one was open for 15% -> 6% of each run, Pallas kernels for 0% -> 10%
where the time goes in v1:
time: 33.8 us; the launch traced here: 33.6 us
  blocking collectives  20.6 us (61%)
  Pallas kernels  7.15 us (21%)
  starting transfers between devices  2.97 us (9%)
  local copies, waits for them, and re-layouts  2.74 us (8%)
    all_to_all x1, blocking collectives, shards(): lax.all_to_all(outgoing, ('fit', 'ao'), split_axis=0, concat_axis=0, tile...  20.6 us
    pallas_call x1, Pallas kernels, shards(): pl.pallas_call(first_step, out_shape=(total_shape, jax.ShapeDtypeStruct((...  3.46 us
    ppermute x1, starting transfers between devices, from_behind(): lax.ppermute(block, axis, [((i - distance) % count, i) for i in range(cou...  2.97 us
    reshape x1, local copies, waits for them, and re-layouts, shards(): tiles = resident.reshape(resident.shape[0], AB, FB)  2.09 us
    pallas_call x1, Pallas kernels, shards(): pl.pallas_call(collect, out_shape=jax.ShapeDtypeStruct((OWN_CAP, height,...  1.86 us
    pallas_call x1, Pallas kernels, shards(): pl.pallas_call(last_step, out_shape=jax.ShapeDtypeStruct((fit_count * ao_...  1.83 us
  transfers between devices with their start and end apart: 1, of which 0 were waited for; matrix products, arithmetic and copies ran while one was open for 6% of the time, Pallas kernels for 10%

profile of v1, /device:TPU:0, one launch (start us, length us, event | category | flops | bytes accessed | tf_op | source)
XLA Modules:
  0.0 33.6 jit_solution(17457360271371833622)
XLA Ops:
  0.0 3.0 %collective-permute-start = (bf16[192,512]{1,0:T(8,128)(2,1)}, bf16[192,512]{1,0:T(8,128)(2,1)S(1)}, u32[]{:S(2)}, u32[]{:S(2)}) collective-permute-start(bf16[192,512]{1,0:T(8,128)(2,1)} %occ_ref.1), channel_id=1, source_target_pairs={{16,0},{0,16},{17,1},{1,17},{18,2},{2,18},{19,3},{3,19},{20,4},{4,... | collective-permute-start | bytes 589832 | tf_op jit(solution)/shard_map/ppermute | solution.py:27
  3.0 0.0 copy-start
  3.0 0.0 copy-start.1
  3.0 0.0 copy-start.5
  3.0 2.1 %reshape.7.tiles_ref = bf16[64,64,64]{2,1,0:T(8,128)(2,1)S(1)} reshape(bf16[64,4096]{1,0:T(8,128)(2,1)} %param.8) | data formatting | bytes 1048576 | tf_op jit(solution)/shard_map/reshape | solution.py:219
  5.1 0.0 copy-start.2
  5.1 0.0 copy-start.3
  5.1 0.0 copy-start.4
  5.1 0.0 copy-done
  5.1 0.0 copy-done.1
  5.1 0.0 copy-done.5
  5.1 0.6 %copy-done.2 = s32[3,1,2,24]{3,2,1,0:T(2,128)S(1)} copy-done((s32[3,1,2,24]{3,2,1,0:T(2,128)S(1)}, s32[3,1,2,24]{3,2,1,0:T(2,128)}, u32[]{:S(2)}) %copy-start.2) | copy-done | bytes 600
  5.8 0.0 copy-done.3
  5.8 0.0 copy-done.4
  5.8 3.5 %shard_map.73 = (f32[32,64,128]{2,1,0:T(8,128)S(1)}, bf16[1,32,64,192]{3,2,1,0:T(8,128)(2,1)S(1)}, s32[32]{0:T(128)S(1)}, s32[16,128]{1,0:T(8,128)S(1)}) custom-call(s32[1]{0:T(128)} %bitcast.column_ref, s32[1,2,24]{2,1,0:T(2,128)S(1)} %copy-done.3, s32[3,1,2,24]{3,2,1,0:T(2,128)S(1)} %copy-done.2, s32[1,2]{1,0:T(1,128)S(1)} %copy-done.4, ...), custom_call_target="tpu_custom_call" | custom-call | tf_op jit(solution)/shard_map/pallas_call | solution.py:221
  9.2 0.0 collective-permute-done.occ_ref
  9.2 1.8 %shard_map.74 = s32[32,32,128]{2,1,0:T(8,128)S(1)} custom-call(s32[32]{0:T(128)S(1)} %get-tuple-element.10.occ_of_ref, bf16[1,32,64,192]{3,2,1,0:T(8,128)(2,1)S(1)} %get-tuple-element.11.later_ref, bf16[192,512]{1,0:T(8,128)(2,1)S(1)} %collective-permute-done.occ_ref, f32[32,64,128]{2,1,0:T(8,128)S(1)} %get-tuple-element.12.before_ref), custom_call_target="tpu_custom_call" | custom-call | tf_op jit(solution)/shard_map/pallas_call | solution.py:249
  11.1 20.6 %all_to_all.5.received_ref = s32[32,32,128]{2,1,0:T(8,128)S(1)} all-to-all(s32[32,32,128]{2,1,0:T(8,128)S(1)} %shard_map.74), channel_id=1, replica_groups=mesh['fit'=2,'ao'=16] {'fit','ao'}, dimensions={0} | all-to-all | bytes 1048576 | tf_op jit(solution)/shard_map/all_to_all | solution.py:255
  31.7 1.9 %shard_map.75 = bf16[8,32,512]{2,1,0:T(8,128)(2,1)} custom-call(s32[16,128]{1,0:T(8,128)S(1)} %get-tuple-element.9.target_ref, s32[32,32,128]{2,1,0:T(8,128)S(1)} %all_to_all.5.received_ref), custom_call_target="tpu_custom_call" | custom-call | tf_op jit(solution)/shard_map/pallas_call | solution.py:256
Async XLA Ops:
  0.0 9.2 %collective-permute-start = (bf16[192,512]{1,0:T(8,128)(2,1)}, bf16[192,512]{1,0:T(8,128)(2,1)S(1)}, u32[]{:S(2)}, u32[]{:S(2)}) collective-permute-start(bf16[192,512]{1,0:T(8,128)(2,1)} %occ_ref.1), channel_id=1, source_target_pairs={{16,0},{0,16},{17,1},{1,17},{18,2},{2,18},{19,3},{3,19},{20,4},{4,... | collective-permute-start | bytes 589832 | tf_op jit(solution)/shard_map/ppermute | solution.py:27
  3.0 2.1 %copy-start = (bf16[192,512]{1,0:T(8,128)(2,1)S(1)}, bf16[192,512]{1,0:T(8,128)(2,1)}, u32[]{:S(2)}) copy-start(bf16[192,512]{1,0:T(8,128)(2,1)} %occ_ref.1) | copy-start | bytes 589828
  3.0 2.2 %copy-start.1 = (s32[16,24]{1,0:T(8,128)S(1)}, s32[16,24]{1,0:T(8,128)}, u32[]{:S(2)}) copy-start(s32[16,24]{1,0:T(8,128)} %list_vec.1) | copy-start | bytes 4612
  3.0 2.2 %copy-start.5 = (s32[64]{0:T(128)S(1)}, s32[64]{0:T(128)}, u32[]{:S(2)}) copy-start(s32[64]{0:T(128)} %slot_ref.1) | copy-start | bytes 772
  5.1 0.7 %copy-start.2 = (s32[3,1,2,24]{3,2,1,0:T(2,128)S(1)}, s32[3,1,2,24]{3,2,1,0:T(2,128)}, u32[]{:S(2)}) copy-start(s32[3,1,2,24]{3,2,1,0:T(2,128)} %pairs_ref.1) | copy-start | bytes 1732
  5.1 0.7 %copy-start.3 = (s32[1,2,24]{2,1,0:T(2,128)S(1)}, s32[1,2,24]{2,1,0:T(2,128)}, u32[]{:S(2)}) copy-start(s32[1,2,24]{2,1,0:T(2,128)} %rows_ref.1) | copy-start | bytes 580
  5.1 0.7 %copy-start.4 = (s32[1,2]{1,0:T(1,128)S(1)}, s32[1,2]{1,0:T(1,128)}, u32[]{:S(2)}) copy-start(s32[1,2]{1,0:T(1,128)} %live_ref.1) | copy-start | bytes 28

commit v2 on v1

--- a/solution.py
+++ b/solution.py
@@ -19,6 +19,7 @@
 LIMIT = 48 * 1024 * 1024
 
 SMEM = pl.BlockSpec(memory_space=pltpu.SMEM)
+HBM = pl.BlockSpec(memory_space=pltpu.HBM)
 VMEM = pl.BlockSpec(memory_space=pltpu.VMEM)
 
 
@@ -27,6 +28,10 @@
     return lax.ppermute(block, axis, [((i - distance) % count, i) for i in range(count)])
 
 
+def in_hbm(array):
+    return pltpu.with_memory_space_constraint(array, pltpu.HBM)
+
+
 def rounded(value):
     return (value + NEAREST) - NEAREST
 
@@ -36,15 +41,25 @@
 
 
 def first_step(
-    column_ref, rows_ref, pairs_ref, live_ref, list_ref, slot_ref, list_vec, tiles_ref, occ_ref,
+    column_ref, list_any, slot_any, rows_any, pairs_any, live_any, resident_any, occ_any,
     total_ref, later_ref, occ_of_ref, target_ref,
-    sid_of_tile, held, pair_of,
+    sid_of_tile, held, pair_of, tiles, targets,
+    list_ref, slot_ref, rows_ref, pairs_ref, live_ref, list_vec, resident_ref, occ_ref, arrived,
 ):
+    sources = (list_any, slot_any, rows_any, pairs_any, live_any, list_any, resident_any, occ_any)
+    landed = (list_ref, slot_ref, rows_ref, pairs_ref, live_ref, list_vec, resident_ref, occ_ref)
+    copies = [
+        pltpu.make_async_copy(source, landing, arrived.at[at])
+        for at, (source, landing) in enumerate(zip(sources, landed))
+    ]
+    for copy in copies:
+        copy.start()
+
     steps, width = rows_ref.shape[1:]
     fit_blocks = pairs_ref.shape[0]
     ao_count = list_ref.shape[0]
     slots = ao_count * CAP
-    pair_step = tiles_ref.shape[0] // steps
+    pair_step = resident_ref.shape[0] // steps
     occ_count = occ_ref.shape[1] // OB
     column = column_ref[0]
 
@@ -60,6 +75,9 @@
 
     lax.fori_loop(0, ao_count, clear_owner, 0, unroll=8)
     lax.fori_loop(0, slots, clear_slot, 0, unroll=8)
+
+    for copy in copies[:2]:
+        copy.wait()
 
     def route(tile, _):
         code = list_ref[column, tile]
@@ -73,6 +91,8 @@
 
     lax.fori_loop(0, width, route, 0, unroll=4)
 
+    for copy in copies[2:5]:
+        copy.wait()
     for step in range(steps):
         live = live_ref[0, step]
 
@@ -88,14 +108,28 @@
 
         lax.fori_loop(0, width, place, 0, unroll=4)
 
+    for copy in copies[5:]:
+        copy.wait()
+    for start in range(0, resident_ref.shape[0], 16):
+        tiles[start : start + 16] = resident_ref[start : start + 16, :].reshape(
+            16, AB * FB // OB, OB
+        )
+
     def tile_at(step, j, slot):
         pair = pair_of[(step * fit_blocks + j) * slots + slot]
-        picked = tiles_ref[jnp.maximum(pair, 0)]
+        picked = tiles[jnp.maximum(pair, 0)]
         return jnp.where(pair >= 0, picked, jnp.zeros_like(picked))
 
     def one_slot(slot, _):
         for step in range(steps):
-            left = jnp.concatenate([tile_at(step, j, slot) for j in range(fit_blocks)], axis=1)
+            picked = [tile_at(step, j, slot) for j in range(fit_blocks)]
+            left = jnp.concatenate(
+                [
+                    jnp.concatenate([tile[:, at : at + FB] for tile in picked], axis=1)
+                    for at in range(0, OB, FB)
+                ],
+                axis=0,
+            )
             if step:
                 later_ref[step - 1, slot] = left
             else:
@@ -119,8 +153,11 @@
     last = jnp.max(jnp.where(mine, key, -1), axis=1, keepdims=True)
     first_goal = jnp.where(last >= 0, first % count, count)
     last_goal = jnp.where(last > first, last % count, count)
-    lane = lax.broadcasted_iota(jnp.int32, target_ref.shape, 1)
-    target_ref[...] = jnp.where(lane == 0, first_goal, last_goal)
+    lane = lax.broadcasted_iota(jnp.int32, targets.shape, 1)
+    targets[...] = jnp.where(lane == 0, first_goal, last_goal)
+    copy = pltpu.make_async_copy(targets, target_ref, arrived.at[0])
+    copy.start()
+    copy.wait()
 
 
 def middle_step(occ_of_ref, later_ref, occ_ref, before_ref, total_ref):
@@ -155,6 +192,13 @@
     return whole.astype(jnp.float32) * scale
 
 
+def rows_of(total, part, height):
+    half = height // 2
+    return jnp.concatenate(
+        [total[at + part * half : at + (part + 1) * half] for at in (0, AB // 2)], axis=0
+    )
+
+
 def last_step(occ_of_ref, later_ref, occ_ref, before_ref, out_ref):
     height = out_ref.shape[1]
     fit_count = AB // height
@@ -173,32 +217,40 @@
                 )
             )
         for part in range(fit_count):
-            low, high = [coded(total[part * height : (part + 1) * height]) for total in sums]
+            low, high = [coded(rows_of(total, part, height)) for total in sums]
             out_ref[part * ao_count + owner] = (low & 0xFFFF) | lax.shift_left(high, 16)
         return 0
 
-    lax.fori_loop(0, ao_count, one_owner, 0, unroll=4)
+    lax.fori_loop(0, ao_count, one_owner, 0, unroll=16)
 
 
 def collect(target_ref, received_ref, out_ref, sums):
     ao_count = target_ref.shape[0]
+    fit_count = received_ref.shape[0] // ao_count
+    height = out_ref.shape[1]
+    half = height // 2
     occ_count = out_ref.shape[2] // OB
     sums[...] = jnp.zeros_like(sums)
 
-    def one_source(source, _):
-        column = lax.rem(source, ao_count)
-        words = received_ref[source]
-        low = lax.shift_right_arithmetic(lax.shift_left(words, 16), 16)
-        high = lax.shift_right_arithmetic(words, 16)
-        first, second = target_ref[column, 0], target_ref[column, 1]
-        sums[first] += decoded(low)
-        sums[second] += decoded(high)
-        return 0
-
-    lax.fori_loop(0, received_ref.shape[0], one_source, 0, unroll=8)
+    def one_column(column, _):
+        lows, highs = [], []
+        for part in range(fit_count):
+            words = received_ref[part * ao_count + column]
+            lows.append(decoded(lax.shift_right_arithmetic(lax.shift_left(words, 16), 16)))
+            highs.append(decoded(lax.shift_right_arithmetic(words, 16)))
+        for rank, parts in enumerate((lows, highs)):
+            total = functools.reduce(jnp.add, parts)
+            start = target_ref[column, rank] * height
+            for odd in range(2):
+                rows = pl.ds(start + odd, half, stride=2)
+                sums[rows, :] += total[odd * half : (odd + 1) * half]
+        return 0
+
+    lax.fori_loop(0, ao_count, one_column, 0, unroll=16)
     for slot in range(OWN_CAP):
         for occ in range(occ_count):
-            out_ref[slot, :, occ * OB : (occ + 1) * OB] = sums[slot * occ_count + occ].astype(
+            start = (slot * occ_count + occ) * height
+            out_ref[slot, :, occ * OB : (occ + 1) * OB] = sums[start : start + height].astype(
                 out_ref.dtype
             )
 
@@ -216,27 +268,34 @@
     params = pltpu.CompilerParams(vmem_limit_bytes=LIMIT)
 
     incoming = from_behind(occ_blocks, "fit", 1)
-    tiles = resident.reshape(resident.shape[0], AB, FB)
+    indices = (tile_list, owner_slot, row_tiles, row_pairs, live_rows)
     total_shape = jax.ShapeDtypeStruct((slots, AB, OB), jnp.float32)
     total, later, occ_of, targets = pl.pallas_call(
         first_step,
         out_shape=(
             total_shape,
             jax.ShapeDtypeStruct((fit_count - 1, slots, AB, depth), jnp.bfloat16),
-            jax.ShapeDtypeStruct((slots,), jnp.int32),
-            jax.ShapeDtypeStruct((ao_count, OB), jnp.int32),
+            pltpu.SMEM((slots,), jnp.int32),
+            pltpu.SMEM((ao_count, OB), jnp.int32),
         ),
-        in_specs=[SMEM] * 6 + [VMEM] * 3,
-        out_specs=(VMEM, VMEM, SMEM, VMEM),
+        in_specs=[SMEM] + [HBM] * 7,
+        out_specs=(VMEM, VMEM, SMEM, SMEM),
         scratch_shapes=[
             pltpu.SMEM((width,), jnp.int32),
             pltpu.SMEM((ao_count,), jnp.int32),
             pltpu.SMEM((fit_count * fit_blocks * slots,), jnp.int32),
+            pltpu.VMEM((resident.shape[0], AB * FB // OB, OB), jnp.bfloat16),
+            pltpu.VMEM((ao_count, OB), jnp.int32),
+            *[pltpu.SMEM(index.shape, index.dtype) for index in indices],
+            *[pltpu.VMEM(block.shape, block.dtype) for block in (tile_list, resident, occ_blocks)],
+            pltpu.SemaphoreType.DMA((len(indices) + 3,)),
         ],
         compiler_params=params,
-    )(column, row_tiles, row_pairs, live_rows, tile_list, owner_slot, tile_list, tiles, occ_blocks)
+    )(column, *[in_hbm(array) for array in (*indices, resident, occ_blocks)])
 
     def step_specs(step):
+        if fit_count == 2:
+            return dict(in_specs=[SMEM, VMEM, VMEM, VMEM], out_specs=VMEM)
         at_step = pl.BlockSpec((None, slots, AB, depth), lambda at: (step - 1, 0, 0, 0))
         return dict(grid=(1,), in_specs=[SMEM, at_step, VMEM, VMEM], out_specs=VMEM)
 
@@ -251,14 +310,14 @@
         out_shape=jax.ShapeDtypeStruct((fit_count * ao_count, height, OB), jnp.int32),
         compiler_params=params,
         **step_specs(fit_count - 1),
-    )(occ_of, later, incoming, total)
+    )(occ_of, later[0] if fit_count == 2 else later, incoming, total)
     received = lax.all_to_all(outgoing, ("fit", "ao"), split_axis=0, concat_axis=0, tiled=True)
     return pl.pallas_call(
         collect,
         out_shape=jax.ShapeDtypeStruct((OWN_CAP, height, occ_count * OB), jnp.bfloat16),
         in_specs=[SMEM, VMEM],
         out_specs=VMEM,
-        scratch_shapes=[pltpu.VMEM((OWN_CAP * occ_count + 1, height, OB), jnp.float32)],
+        scratch_shapes=[pltpu.VMEM(((OWN_CAP * occ_count + 1) * height, OB), jnp.float32)],
         compiler_params=params,
     )(targets, received)
 

time: 33.8 us -> 31.9 us (0.944)
  local copies, waits for them, and re-layouts: 2.74 us -> 0 us
  Pallas kernels: 7.15 us -> 5.74 us
  blocking collectives: 20.6 us -> 21.8 us
  waiting for transfers between devices: 0.01 us -> 1.2 us
    reshape x1 -> x0, local copies, waits for them, and re-layouts: 2.09 us -> none  [shards(): tiles = resident.reshape(resident.shape[0], AB, FB)]
    ppermute x1, waiting for transfers between devices: 0.01 us -> 1.2 us  [from_behind(): lax.ppermute(block, axis, [((i - distance) % count, i) for i in range(cou...]
    all_to_all x1, blocking collectives: 20.6 us -> 21.8 us  [shards(): lax.all_to_all(outgoing, ('fit', 'ao'), split_axis=0, concat_axis=0, tile...]
    pallas_call x1, Pallas kernels: 1.83 us -> 0.83 us  [shards(): pl.pallas_call(last_step, out_shape=jax.ShapeDtypeStruct((fit_count * ao_...]
    pallas_call x1, Pallas kernels: 1.86 us -> 1.02 us  [shards(): pl.pallas_call(collect, out_shape=jax.ShapeDtypeStruct((OWN_CAP, height,...]
    unnamed x12 -> x0, local copies, waits for them, and re-layouts: 0.65 us -> none
    pallas_call x1, Pallas kernels: 3.46 us -> 3.9 us  [shards(): pl.pallas_call(first_step, out_shape=(total_shape, jax.ShapeDtypeStruct((...]
  transfers between devices with their start and end apart: 1 -> 1, of which waited for: 0 -> 1; matrix products, arithmetic and copies ran while one was open for 6% -> 0% of each run, Pallas kernels for 10% -> 12%
where the time goes in v2:
time: 31.9 us; the launch traced here: 31.7 us
  blocking collectives  21.8 us (68%)
  Pallas kernels  5.74 us (18%)
  starting transfers between devices  2.97 us (9%)
  waiting for transfers between devices  1.2 us (4%)
    all_to_all x1, blocking collectives, shards(): lax.all_to_all(outgoing, ('fit', 'ao'), split_axis=0, concat_axis=0, tile...  21.8 us
    pallas_call x1, Pallas kernels, shards(): pl.pallas_call(first_step, out_shape=(total_shape, jax.ShapeDtypeStruct((...  3.9 us
    ppermute x1, starting transfers between devices, from_behind(): lax.ppermute(block, axis, [((i - distance) % count, i) for i in range(cou...  2.97 us
    ppermute x1, waiting for transfers between devices, from_behind(): lax.ppermute(block, axis, [((i - distance) % count, i) for i in range(cou...  1.2 us
    pallas_call x1, Pallas kernels, shards(): pl.pallas_call(collect, out_shape=jax.ShapeDtypeStruct((OWN_CAP, height,...  1.02 us
    pallas_call x1, Pallas kernels, shards(): pl.pallas_call(last_step, out_shape=jax.ShapeDtypeStruct((fit_count * ao_...  0.83 us
  transfers between devices with their start and end apart: 1, of which 1 were waited for; matrix products, arithmetic and copies ran while one was open for 0% of the time, Pallas kernels for 12%

profile of v2, /device:TPU:0, one launch (start us, length us, event | category | flops | bytes accessed | tf_op | source)
XLA Modules:
  0.0 31.7 jit_solution(12552164823563039237)
XLA Ops:
  0.0 3.0 %collective-permute-start = (bf16[192,512]{1,0:T(8,128)(2,1)}, bf16[192,512]{1,0:T(8,128)(2,1)S(1)}, u32[]{:S(2)}, u32[]{:S(2)}) collective-permute-start(bf16[192,512]{1,0:T(8,128)(2,1)} %occ_any.1), channel_id=1, source_target_pairs={{16,0},{0,16},{17,1},{1,17},{18,2},{2,18},{19,3},{3,19},{20,4},{4,... | collective-permute-start | bytes 589832 | tf_op jit(solution)/shard_map/ppermute | solution.py:28
  3.0 3.9 %shard_map.73 = (f32[32,64,128]{2,1,0:T(8,128)S(1)}, bf16[1,32,64,192]{3,2,1,0:T(8,128)(2,1)S(1)}, s32[32]{0:T(128)S(4)}, s32[16,128]{1,0:T(8,128)S(4)}) custom-call(s32[1]{0:T(128)} %bitcast.column_ref, s32[16,24]{1,0:T(8,128)} %list_any.1, s32[64]{0:T(128)} %slot_any.1, s32[1,2,24]{2,1,0:T(2,128)} %rows_any.1, s32[3,1,2,24]{3,2,1,0:T(2,128)} %pairs_any.1, ...), custom_call_target="tpu_custom_call" | custom-call | tf_op jit(solution)/shard_map/pallas_call | solution.py:273
  6.9 1.2 %collective-permute-done.occ_ref = bf16[192,512]{1,0:T(8,128)(2,1)S(1)} collective-permute-done((bf16[192,512]{1,0:T(8,128)(2,1)}, bf16[192,512]{1,0:T(8,128)(2,1)S(1)}, u32[]{:S(2)}, u32[]{:S(2)}) %collective-permute-start) | collective-permute-done | bytes 196640 | tf_op jit(solution)/shard_map/ppermute | solution.py:28
  8.1 0.8 %shard_map.74 = s32[32,32,128]{2,1,0:T(8,128)S(1)} custom-call(s32[32]{0:T(128)S(4)} %get-tuple-element.10.occ_of_ref, bf16[32,64,192]{2,1,0:T(8,128)(2,1)S(1)} %bitcast.2, bf16[192,512]{1,0:T(8,128)(2,1)S(1)} %collective-permute-done.occ_ref, f32[32,64,128]{2,1,0:T(8,128)S(1)} %get-tuple-element.12.before_ref), custom_call_target="tpu_custom_call" | custom-call | tf_op jit(solution)/shard_map/pallas_call | solution.py:308
  8.9 21.8 %all_to_all.5.received_ref = s32[32,32,128]{2,1,0:T(8,128)S(1)} all-to-all(s32[32,32,128]{2,1,0:T(8,128)S(1)} %shard_map.74), channel_id=1, replica_groups=mesh['fit'=2,'ao'=16] {'fit','ao'}, dimensions={0} | all-to-all | bytes 1048576 | tf_op jit(solution)/shard_map/all_to_all | solution.py:314
  30.7 1.0 %shard_map.75 = bf16[8,32,512]{2,1,0:T(8,128)(2,1)} custom-call(s32[16,128]{1,0:T(8,128)S(4)} %get-tuple-element.9.target_ref, s32[32,32,128]{2,1,0:T(8,128)S(1)} %all_to_all.5.received_ref), custom_call_target="tpu_custom_call" | custom-call | tf_op jit(solution)/shard_map/pallas_call | solution.py:315
Async XLA Ops:
  0.0 8.1 %collective-permute-start = (bf16[192,512]{1,0:T(8,128)(2,1)}, bf16[192,512]{1,0:T(8,128)(2,1)S(1)}, u32[]{:S(2)}, u32[]{:S(2)}) collective-permute-start(bf16[192,512]{1,0:T(8,128)(2,1)} %occ_any.1), channel_id=1, source_target_pairs={{16,0},{0,16},{17,1},{1,17},{18,2},{2,18},{19,3},{3,19},{20,4},{4,... | collective-permute-start | bytes 589832 | tf_op jit(solution)/shard_map/ppermute | solution.py:28

commit v3 on v2

--- a/solution.py
+++ b/solution.py
@@ -18,6 +18,9 @@
 NEAREST = 12582912.0
 LIMIT = 48 * 1024 * 1024
 
+AO = ("ao3", "ao2", "ao1", "ao0")
+ORDER = ('ao0', 'ao2', 'fit', 'ao1', 'ao3')
+
 SMEM = pl.BlockSpec(memory_space=pltpu.SMEM)
 HBM = pl.BlockSpec(memory_space=pltpu.HBM)
 VMEM = pl.BlockSpec(memory_space=pltpu.VMEM)
@@ -26,6 +29,17 @@
 def from_behind(block, axis, distance):
     count = lax.axis_size(axis)
     return lax.ppermute(block, axis, [((i - distance) % count, i) for i in range(count)])
+
+
+def place(fit, ao, sizes):
+    at = {"fit": fit}
+    for axis in reversed(AO):
+        at[axis] = lax.rem(ao, sizes[axis])
+        ao = lax.div(ao, sizes[axis])
+    position = 0
+    for axis in ORDER:
+        position = position * sizes[axis] + at[axis]
+    return position
 
 
 def in_hbm(array):
@@ -131,7 +145,8 @@
                 axis=0,
             )
             if step:
-                later_ref[step - 1, slot] = left
+                spare = jnp.zeros((AB, later_ref.shape[3] - left.shape[1]), left.dtype)
+                later_ref[step - 1, slot] = jnp.concatenate([left, spare], axis=1)
             else:
                 total_ref[slot] = jnp.dot(
                     left, occ_columns(occ_ref, occ_of_ref[slot]), preferred_element_type=jnp.float32
@@ -160,7 +175,15 @@
     copy.wait()
 
 
-def middle_step(occ_of_ref, later_ref, occ_ref, before_ref, total_ref):
+def padded(occ_in, occ_ref):
+    rows = occ_in.shape[0]
+    occ_ref[:rows] = occ_in[...]
+    occ_ref[rows:] = jnp.zeros((occ_ref.shape[0] - rows, occ_ref.shape[1]), occ_ref.dtype)
+
+
+def middle_step(occ_of_ref, later_ref, occ_in, before_ref, total_ref, occ_ref):
+    padded(occ_in, occ_ref)
+
     def one_slot(slot, _):
         total_ref[slot] = before_ref[slot] + jnp.dot(
             later_ref[slot], occ_columns(occ_ref, occ_of_ref[slot]), preferred_element_type=jnp.float32
@@ -199,7 +222,8 @@
     )
 
 
-def last_step(occ_of_ref, later_ref, occ_ref, before_ref, out_ref):
+def last_step(sizes, occ_of_ref, later_ref, occ_in, before_ref, out_ref, occ_ref):
+    padded(occ_in, occ_ref)
     height = out_ref.shape[1]
     fit_count = AB // height
     ao_count = out_ref.shape[0] // fit_count
@@ -218,13 +242,13 @@
             )
         for part in range(fit_count):
             low, high = [coded(rows_of(total, part, height)) for total in sums]
-            out_ref[part * ao_count + owner] = (low & 0xFFFF) | lax.shift_left(high, 16)
+            out_ref[place(part, owner, sizes)] = (low & 0xFFFF) | lax.shift_left(high, 16)
         return 0
 
     lax.fori_loop(0, ao_count, one_owner, 0, unroll=16)
 
 
-def collect(target_ref, received_ref, out_ref, sums):
+def collect(sizes, target_ref, received_ref, out_ref, sums):
     ao_count = target_ref.shape[0]
     fit_count = received_ref.shape[0] // ao_count
     height = out_ref.shape[1]
@@ -235,7 +259,7 @@
     def one_column(column, _):
         lows, highs = [], []
         for part in range(fit_count):
-            words = received_ref[part * ao_count + column]
+            words = received_ref[place(part, column, sizes)]
             lows.append(decoded(lax.shift_right_arithmetic(lax.shift_left(words, 16), 16)))
             highs.append(decoded(lax.shift_right_arithmetic(words, 16)))
         for rank, parts in enumerate((lows, highs)):
@@ -257,14 +281,15 @@
 
 def shards(occ_blocks, resident, row_tiles, row_pairs, live_rows, tile_list, owner_slot):
     fit_count = lax.axis_size("fit")
-    ao_count = lax.axis_size("ao")
+    sizes = {axis: lax.axis_size(axis) for axis in ORDER}
+    ao_count = lax.axis_size(AO)
     fit_blocks = row_pairs.shape[0]
-    depth = fit_blocks * FB
+    depth = -(-fit_blocks * FB // 256) * 256
     width = tile_list.shape[1]
     slots = ao_count * CAP
     height = AB // fit_count
     occ_count = occ_blocks.shape[1] // OB
-    column = lax.axis_index("ao").astype(jnp.int32).reshape(1)
+    column = lax.axis_index(AO).astype(jnp.int32).reshape(1)
     params = pltpu.CompilerParams(vmem_limit_bytes=LIMIT)
 
     incoming = from_behind(occ_blocks, "fit", 1)
@@ -293,11 +318,15 @@
         compiler_params=params,
     )(column, *[in_hbm(array) for array in (*indices, resident, occ_blocks)])
 
+    wide = [pltpu.VMEM((depth, occ_blocks.shape[1]), occ_blocks.dtype)]
+
     def step_specs(step):
         if fit_count == 2:
-            return dict(in_specs=[SMEM, VMEM, VMEM, VMEM], out_specs=VMEM)
+            return dict(in_specs=[SMEM, VMEM, VMEM, VMEM], out_specs=VMEM, scratch_shapes=wide)
         at_step = pl.BlockSpec((None, slots, AB, depth), lambda at: (step - 1, 0, 0, 0))
-        return dict(grid=(1,), in_specs=[SMEM, at_step, VMEM, VMEM], out_specs=VMEM)
+        return dict(
+            grid=(1,), in_specs=[SMEM, at_step, VMEM, VMEM], out_specs=VMEM, scratch_shapes=wide
+        )
 
     for step in range(1, fit_count - 1):
         total = pl.pallas_call(
@@ -306,14 +335,14 @@
         incoming = from_behind(incoming, "fit", 1)
 
     outgoing = pl.pallas_call(
-        last_step,
+        functools.partial(last_step, sizes),
         out_shape=jax.ShapeDtypeStruct((fit_count * ao_count, height, OB), jnp.int32),
         compiler_params=params,
         **step_specs(fit_count - 1),
     )(occ_of, later[0] if fit_count == 2 else later, incoming, total)
-    received = lax.all_to_all(outgoing, ("fit", "ao"), split_axis=0, concat_axis=0, tiled=True)
+    received = lax.all_to_all(outgoing, ORDER, split_axis=0, concat_axis=0, tiled=True)
     return pl.pallas_call(
-        collect,
+        functools.partial(collect, sizes),
         out_shape=jax.ShapeDtypeStruct((OWN_CAP, height, occ_count * OB), jnp.bfloat16),
         in_specs=[SMEM, VMEM],
         out_specs=VMEM,
@@ -323,18 +352,21 @@
 
 
 def solution(mesh):
+    fit_count, ao_count = mesh.devices.shape
+    parts = mesh.devices.reshape(fit_count, ao_count // 8, 2, 2, 2)
+    every = ("fit", *AO)
     return jax.shard_map(
         shards,
-        mesh=mesh,
+        mesh=jax.sharding.Mesh(parts, every),
         in_specs=(
-            P(("fit", "ao"), None),
-            P(("fit", "ao"), None),
-            P(("fit", "ao"), None, None),
-            P(None, ("fit", "ao"), None, None),
-            P(("fit", "ao"), None),
+            P(every, None),
+            P(every, None),
+            P(every, None, None),
+            P(None, every, None, None),
+            P(every, None),
             P(),
             P(),
         ),
-        out_specs=P("ao", "fit", None),
+        out_specs=P(AO, "fit", None),
         check_vma=False,
     )

time: 31.9 us -> 30.9 us (0.969)
  blocking collectives: 21.8 us -> 20.6 us
    all_to_all x1, blocking collectives: 21.8 us -> 20.6 us  [shards(): lax.all_to_all(outgoing, ORDER, split_axis=0, concat_axis=0, tiled=True)]
  transfers between devices with their start and end apart: 1 -> 1, of which waited for: 1 -> 1; matrix products, arithmetic and copies ran while one was open for 0% -> 0% of each run, Pallas kernels for 12% -> 13%
where the time goes in v3:
time: 30.9 us; the launch traced here: 30.5 us
  blocking collectives  20.6 us (67%)
  Pallas kernels  5.67 us (18%)
  starting transfers between devices  2.97 us (10%)
  waiting for transfers between devices  1.2 us (4%)
    all_to_all x1, blocking collectives, shards(): lax.all_to_all(outgoing, ORDER, split_axis=0, concat_axis=0, tiled=True)  20.6 us
    pallas_call x1, Pallas kernels, shards(): pl.pallas_call(first_step, out_shape=(total_shape, jax.ShapeDtypeStruct((...  3.9 us
    ppermute x1, starting transfers between devices, from_behind(): lax.ppermute(block, axis, [((i - distance) % count, i) for i in range(cou...  2.97 us
    ppermute x1, waiting for transfers between devices, from_behind(): lax.ppermute(block, axis, [((i - distance) % count, i) for i in range(cou...  1.2 us
    pallas_call x1, Pallas kernels, shards(): pl.pallas_call(functools.partial(collect, sizes), out_shape=jax.ShapeDtyp...  1.02 us
    pallas_call x1, Pallas kernels, shards(): pl.pallas_call(functools.partial(last_step, sizes), out_shape=jax.ShapeDt...  0.75 us
  transfers between devices with their start and end apart: 1, of which 1 were waited for; matrix products, arithmetic and copies ran while one was open for 0% of the time, Pallas kernels for 13%

profile of v3, /device:TPU:0, one launch (start us, length us, event | category | flops | bytes accessed | tf_op | source)
XLA Modules:
  0.0 30.5 jit_solution(5892231605758172635)
XLA Ops:
  0.0 3.0 %collective-permute-start = (bf16[192,512]{1,0:T(8,128)(2,1)}, bf16[192,512]{1,0:T(8,128)(2,1)S(1)}, u32[]{:S(2)}, u32[]{:S(2)}) collective-permute-start(bf16[192,512]{1,0:T(8,128)(2,1)} %occ_any.1), channel_id=1, source_target_pairs={{16,0},{0,16},{17,1},{1,17},{18,2},{2,18},{19,3},{3,19},{20,4},{4,... | collective-permute-start | bytes 589832 | tf_op jit(solution)/shard_map/ppermute | solution.py:31
  3.0 3.9 %shard_map.73 = (f32[32,64,128]{2,1,0:T(8,128)S(1)}, bf16[1,32,64,256]{3,2,1,0:T(8,128)(2,1)S(1)}, s32[32]{0:T(128)S(4)}, s32[16,128]{1,0:T(8,128)S(4)}) custom-call(s32[1]{0:T(128)} %bitcast.column_ref, s32[16,24]{1,0:T(8,128)} %list_any.1, s32[64]{0:T(128)} %slot_any.1, s32[1,2,24]{2,1,0:T(2,128)} %rows_any.1, s32[3,1,2,24]{3,2,1,0:T(2,128)} %pairs_any.1, ...), custom_call_target="tpu_custom_call" | custom-call | tf_op jit(solution)/shard_map/pallas_call | solution.py:298
  6.9 1.2 %collective-permute-done.occ_in = bf16[192,512]{1,0:T(8,128)(2,1)S(1)} collective-permute-done((bf16[192,512]{1,0:T(8,128)(2,1)}, bf16[192,512]{1,0:T(8,128)(2,1)S(1)}, u32[]{:S(2)}, u32[]{:S(2)}) %collective-permute-start) | collective-permute-done | bytes 196640 | tf_op jit(solution)/shard_map/ppermute | solution.py:31
  8.1 0.8 %shard_map.74 = s32[32,32,128]{2,1,0:T(8,128)S(1)} custom-call(s32[32]{0:T(128)S(4)} %get-tuple-element.10.occ_of_ref, bf16[32,64,256]{2,1,0:T(8,128)(2,1)S(1)} %bitcast.2, bf16[192,512]{1,0:T(8,128)(2,1)S(1)} %collective-permute-done.occ_in, f32[32,64,128]{2,1,0:T(8,128)S(1)} %get-tuple-element.12.before_ref), custom_call_target="tpu_custom_call" | custom-call | tf_op jit(solution)/shard_map/pallas_call | solution.py:337
  8.8 20.6 %all_to_all.5.received_ref = s32[32,32,128]{2,1,0:T(8,128)S(1)} all-to-all(s32[32,32,128]{2,1,0:T(8,128)S(1)} %shard_map.74), channel_id=1, replica_groups=mesh['fit'=2,'ao3'=2,'ao2'=2,'ao1'=2,'ao0'=2] {'ao0','ao2','fit','ao1','..., dimensions={0} | all-to-all | bytes 1048576 | tf_op jit(solution)/shard_map/all_to_all | solution.py:343
  29.4 1.0 %shard_map.75 = bf16[8,32,512]{2,1,0:T(8,128)(2,1)} custom-call(s32[16,128]{1,0:T(8,128)S(4)} %get-tuple-element.9.target_ref, s32[32,32,128]{2,1,0:T(8,128)S(1)} %all_to_all.5.received_ref), custom_call_target="tpu_custom_call" | custom-call | tf_op jit(solution)/shard_map/pallas_call | solution.py:344
Async XLA Ops:
  0.0 8.1 %collective-permute-start = (bf16[192,512]{1,0:T(8,128)(2,1)}, bf16[192,512]{1,0:T(8,128)(2,1)S(1)}, u32[]{:S(2)}, u32[]{:S(2)}) collective-permute-start(bf16[192,512]{1,0:T(8,128)(2,1)} %occ_any.1), channel_id=1, source_target_pairs={{16,0},{0,16},{17,1},{1,17},{18,2},{2,18},{19,3},{3,19},{20,4},{4,... | collective-permute-start | bytes 589832 | tf_op jit(solution)/shard_map/ppermute | solution.py:31

commit v4 on v2

--- a/solution.py
+++ b/solution.py
@@ -14,9 +14,14 @@
 CAP = 2
 LEVELS = 32700.0
 LOWEST = -100.0
-BIAS = 127.0
+BIAS = -LOWEST
 NEAREST = 12582912.0
 LIMIT = 48 * 1024 * 1024
+
+TURNS = (
+    12, 23, 10, 1, 7, 26, 22, 25, 27, 0, 19, 24, 8, 9, 5, 13, 11, 2, 21, 4, 16, 30, 20, 6,
+    14, 17, 28, 18, 29, 3, 31, 15,
+)
 
 SMEM = pl.BlockSpec(memory_space=pltpu.SMEM)
 HBM = pl.BlockSpec(memory_space=pltpu.HBM)
@@ -26,6 +31,10 @@
 def from_behind(block, axis, distance):
     count = lax.axis_size(axis)
     return lax.ppermute(block, axis, [((i - distance) % count, i) for i in range(count)])
+
+
+def partners(count):
+    return TURNS if count == len(TURNS) else tuple(range(count))
 
 
 def in_hbm(array):
@@ -131,7 +140,8 @@
                 axis=0,
             )
             if step:
-                later_ref[step - 1, slot] = left
+                spare = jnp.zeros((AB, later_ref.shape[3] - left.shape[1]), left.dtype)
+                later_ref[step - 1, slot] = jnp.concatenate([left, spare], axis=1)
             else:
                 total_ref[slot] = jnp.dot(
                     left, occ_columns(occ_ref, occ_of_ref[slot]), preferred_element_type=jnp.float32
@@ -160,7 +170,15 @@
     copy.wait()
 
 
-def middle_step(occ_of_ref, later_ref, occ_ref, before_ref, total_ref):
+def padded(occ_in, occ_ref):
+    rows = occ_in.shape[0]
+    occ_ref[:rows] = occ_in[...]
+    occ_ref[rows:] = jnp.zeros((occ_ref.shape[0] - rows, occ_ref.shape[1]), occ_ref.dtype)
+
+
+def middle_step(occ_of_ref, later_ref, occ_in, before_ref, total_ref, occ_ref):
+    padded(occ_in, occ_ref)
+
     def one_slot(slot, _):
         total_ref[slot] = before_ref[slot] + jnp.dot(
             later_ref[slot], occ_columns(occ_ref, occ_of_ref[slot]), preferred_element_type=jnp.float32
@@ -199,12 +217,13 @@
     )
 
 
-def last_step(occ_of_ref, later_ref, occ_ref, before_ref, out_ref):
+def last_step(turns, occ_of_ref, later_ref, occ_in, before_ref, out_ref, occ_ref):
+    padded(occ_in, occ_ref)
     height = out_ref.shape[1]
     fit_count = AB // height
     ao_count = out_ref.shape[0] // fit_count
 
-    def one_owner(owner, _):
+    def one_owner(owner):
         sums = []
         for rank in range(CAP):
             slot = owner * CAP + rank
@@ -218,13 +237,14 @@
             )
         for part in range(fit_count):
             low, high = [coded(rows_of(total, part, height)) for total in sums]
-            out_ref[part * ao_count + owner] = (low & 0xFFFF) | lax.shift_left(high, 16)
-        return 0
-
-    lax.fori_loop(0, ao_count, one_owner, 0, unroll=16)
-
-
-def collect(target_ref, received_ref, out_ref, sums):
+            out_ref[turns.index(part * ao_count + owner)] = (low & 0xFFFF) | lax.shift_left(high, 16)
+        return 0
+
+    for owner in range(ao_count):
+        one_owner(owner)
+
+
+def collect(turns, target_ref, received_ref, out_ref, sums):
     ao_count = target_ref.shape[0]
     fit_count = received_ref.shape[0] // ao_count
     height = out_ref.shape[1]
@@ -232,10 +252,10 @@
     occ_count = out_ref.shape[2] // OB
     sums[...] = jnp.zeros_like(sums)
 
-    def one_column(column, _):
+    def one_column(column):
         lows, highs = [], []
         for part in range(fit_count):
-            words = received_ref[part * ao_count + column]
+            words = received_ref[turns.index(part * ao_count + column)]
             lows.append(decoded(lax.shift_right_arithmetic(lax.shift_left(words, 16), 16)))
             highs.append(decoded(lax.shift_right_arithmetic(words, 16)))
         for rank, parts in enumerate((lows, highs)):
@@ -246,7 +266,8 @@
                 sums[rows, :] += total[odd * half : (odd + 1) * half]
         return 0
 
-    lax.fori_loop(0, ao_count, one_column, 0, unroll=16)
+    for column in range(ao_count):
+        one_column(column)
     for slot in range(OWN_CAP):
         for occ in range(occ_count):
             start = (slot * occ_count + occ) * height
@@ -258,8 +279,9 @@
 def shards(occ_blocks, resident, row_tiles, row_pairs, live_rows, tile_list, owner_slot):
     fit_count = lax.axis_size("fit")
     ao_count = lax.axis_size("ao")
+    turns = partners(fit_count * ao_count)
     fit_blocks = row_pairs.shape[0]
-    depth = fit_blocks * FB
+    depth = -(-fit_blocks * FB // 256) * 256
     width = tile_list.shape[1]
     slots = ao_count * CAP
     height = AB // fit_count
@@ -293,11 +315,15 @@
         compiler_params=params,
     )(column, *[in_hbm(array) for array in (*indices, resident, occ_blocks)])
 
+    wide = [pltpu.VMEM((depth, occ_blocks.shape[1]), occ_blocks.dtype)]
+
     def step_specs(step):
         if fit_count == 2:
-            return dict(in_specs=[SMEM, VMEM, VMEM, VMEM], out_specs=VMEM)
+            return dict(in_specs=[SMEM, VMEM, VMEM, VMEM], out_specs=VMEM, scratch_shapes=wide)
         at_step = pl.BlockSpec((None, slots, AB, depth), lambda at: (step - 1, 0, 0, 0))
-        return dict(grid=(1,), in_specs=[SMEM, at_step, VMEM, VMEM], out_specs=VMEM)
+        return dict(
+            grid=(1,), in_specs=[SMEM, at_step, VMEM, VMEM], out_specs=VMEM, scratch_shapes=wide
+        )
 
     for step in range(1, fit_count - 1):
         total = pl.pallas_call(
@@ -306,18 +332,25 @@
         incoming = from_behind(incoming, "fit", 1)
 
     outgoing = pl.pallas_call(
-        last_step,
+        functools.partial(last_step, turns),
         out_shape=jax.ShapeDtypeStruct((fit_count * ao_count, height, OB), jnp.int32),
         compiler_params=params,
         **step_specs(fit_count - 1),
     )(occ_of, later[0] if fit_count == 2 else later, incoming, total)
-    received = lax.all_to_all(outgoing, ("fit", "ao"), split_axis=0, concat_axis=0, tiled=True)
+    received = lax.all_to_all(
+        outgoing,
+        ("fit", "ao"),
+        split_axis=0,
+        concat_axis=0,
+        tiled=True,
+        axis_index_groups=[list(turns)],
+    )
     return pl.pallas_call(
-        collect,
+        functools.partial(collect, turns),
         out_shape=jax.ShapeDtypeStruct((OWN_CAP, height, occ_count * OB), jnp.bfloat16),
         in_specs=[SMEM, VMEM],
         out_specs=VMEM,
-        scratch_shapes=[pltpu.VMEM(((OWN_CAP * occ_count + 1) * height, OB), jnp.float32)],
+        scratch_shapes=[pltpu.VMEM(((OWN_CAP * occ_count + 1) * height + 8, OB), jnp.float32)],
         compiler_params=params,
     )(targets, received)
 

time: 31.9 us -> 29.9 us (0.937)
  the two profiles are of different devices: /device:TPU:0 before, /device:TPU:3 now
where the time goes in v4:
time: 29.9 us; the launch traced here: 29.7 us
  blocking collectives  21.9 us (73%)
  Pallas kernels  5.67 us (19%)
  starting transfers between devices  1.24 us (4%)
  waiting for transfers between devices  0.84 us (3%)
    all_to_all x1, blocking collectives, shards(): lax.all_to_all(outgoing, ('fit', 'ao'), split_axis=0, concat_axis=0, tile...  21.9 us
    pallas_call x1, Pallas kernels, shards(): pl.pallas_call(first_step, out_shape=(total_shape, jax.ShapeDtypeStruct((...  3.9 us
    ppermute x1, starting transfers between devices, from_behind(): lax.ppermute(block, axis, [((i - distance) % count, i) for i in range(cou...  1.24 us
    pallas_call x1, Pallas kernels, shards(): pl.pallas_call(functools.partial(collect, turns), out_shape=jax.ShapeDtyp...  1.02 us
    ppermute x1, waiting for transfers between devices, from_behind(): lax.ppermute(block, axis, [((i - distance) % count, i) for i in range(cou...  0.84 us
    pallas_call x1, Pallas kernels, shards(): pl.pallas_call(functools.partial(last_step, turns), out_shape=jax.ShapeDt...  0.75 us
  transfers between devices with their start and end apart: 1, of which 1 were waited for; matrix products, arithmetic and copies ran while one was open for 0% of the time, Pallas kernels for 13%

profile of v4, /device:TPU:3, one launch (start us, length us, event | category | flops | bytes accessed | tf_op | source)
XLA Modules:
  0.0 29.7 jit_solution(8252900612778336918)
XLA Ops:
  0.0 1.2 %collective-permute-start = (bf16[192,512]{1,0:T(8,128)(2,1)}, bf16[192,512]{1,0:T(8,128)(2,1)S(1)}, u32[]{:S(2)}, u32[]{:S(2)}) collective-permute-start(bf16[192,512]{1,0:T(8,128)(2,1)} %occ_any.1), channel_id=1, source_target_pairs={{16,0},{0,16},{17,1},{1,17},{18,2},{2,18},{19,3},{3,19},{20,4},{4,... | collective-permute-start | bytes 589832 | tf_op jit(solution)/shard_map/ppermute | solution.py:33
  1.2 3.9 %shard_map.73 = (f32[32,64,128]{2,1,0:T(8,128)S(1)}, bf16[1,32,64,256]{3,2,1,0:T(8,128)(2,1)S(1)}, s32[32]{0:T(128)S(4)}, s32[16,128]{1,0:T(8,128)S(4)}) custom-call(s32[1]{0:T(128)} %bitcast.column_ref, s32[16,24]{1,0:T(8,128)} %list_any.1, s32[64]{0:T(128)} %slot_any.1, s32[1,2,24]{2,1,0:T(2,128)} %rows_any.1, s32[3,1,2,24]{3,2,1,0:T(2,128)} %pairs_any.1, ...), custom_call_target="tpu_custom_call" | custom-call | tf_op jit(solution)/shard_map/pallas_call | solution.py:295
  5.1 0.8 %collective-permute-done.occ_in = bf16[192,512]{1,0:T(8,128)(2,1)S(1)} collective-permute-done((bf16[192,512]{1,0:T(8,128)(2,1)}, bf16[192,512]{1,0:T(8,128)(2,1)S(1)}, u32[]{:S(2)}, u32[]{:S(2)}) %collective-permute-start) | collective-permute-done | bytes 196640 | tf_op jit(solution)/shard_map/ppermute | solution.py:33
  6.0 0.8 %shard_map.74 = s32[32,32,128]{2,1,0:T(8,128)S(1)} custom-call(s32[32]{0:T(128)S(4)} %get-tuple-element.10.occ_of_ref, bf16[32,64,256]{2,1,0:T(8,128)(2,1)S(1)} %bitcast.2, bf16[192,512]{1,0:T(8,128)(2,1)S(1)} %collective-permute-done.occ_in, f32[32,64,128]{2,1,0:T(8,128)S(1)} %get-tuple-element.12.before_ref), custom_call_target="tpu_custom_call" | custom-call | tf_op jit(solution)/shard_map/pallas_call | solution.py:334
  6.7 21.9 %all_to_all.5.received_ref = s32[32,32,128]{2,1,0:T(8,128)S(1)} all-to-all(s32[32,32,128]{2,1,0:T(8,128)S(1)} %shard_map.74), channel_id=1, replica_groups={{12,23,10,1,7,26,22,25,27,0,19,24,8,9,5,13,11,2,21,4,16,30,20,6,14,17,2..., dimensions={0} | all-to-all | bytes 1048576 | tf_op jit(solution)/shard_map/all_to_all | solution.py:340
  28.7 1.0 %shard_map.75 = bf16[8,32,512]{2,1,0:T(8,128)(2,1)} custom-call(s32[16,128]{1,0:T(8,128)S(4)} %get-tuple-element.9.target_ref, s32[32,32,128]{2,1,0:T(8,128)S(1)} %all_to_all.5.received_ref), custom_call_target="tpu_custom_call" | custom-call | tf_op jit(solution)/shard_map/pallas_call | solution.py:348
Async XLA Ops:
  0.0 6.0 %collective-permute-start = (bf16[192,512]{1,0:T(8,128)(2,1)}, bf16[192,512]{1,0:T(8,128)(2,1)S(1)}, u32[]{:S(2)}, u32[]{:S(2)}) collective-permute-start(bf16[192,512]{1,0:T(8,128)(2,1)} %occ_any.1), channel_id=1, source_target_pairs={{16,0},{0,16},{17,1},{1,17},{18,2},{2,18},{19,3},{3,19},{20,4},{4,... | collective-permute-start | bytes 589832 | tf_op jit(solution)/shard_map/ppermute | solution.py:33

commit v5 on v4

--- a/solution.py
+++ b/solution.py
@@ -19,8 +19,8 @@
 LIMIT = 48 * 1024 * 1024
 
 TURNS = (
-    12, 23, 10, 1, 7, 26, 22, 25, 27, 0, 19, 24, 8, 9, 5, 13, 11, 2, 21, 4, 16, 30, 20, 6,
-    14, 17, 28, 18, 29, 3, 31, 15,
+    12, 21, 10, 1, 7, 26, 22, 24, 27, 0, 6, 25, 8, 9, 5, 15, 11, 2, 13, 3, 16, 23, 20, 19,
+    14, 18, 28, 17, 4, 29, 31, 30,
 )
 
 SMEM = pl.BlockSpec(memory_space=pltpu.SMEM)

time: 29.9 us -> 29.5 us (0.987)
  the two profiles are of different devices: /device:TPU:3 before, /device:TPU:0 now
where the time goes in v5:
time: 29.5 us; the launch traced here: 29.3 us
  blocking collectives  19.4 us (66%)
  Pallas kernels  5.72 us (19%)
  starting transfers between devices  2.97 us (10%)
  waiting for transfers between devices  1.2 us (4%)
    all_to_all x1, blocking collectives, shards(): lax.all_to_all(outgoing, ('fit', 'ao'), split_axis=0, concat_axis=0, tile...  19.4 us
    pallas_call x1, Pallas kernels, shards(): pl.pallas_call(first_step, out_shape=(total_shape, jax.ShapeDtypeStruct((...  3.9 us
    ppermute x1, starting transfers between devices, from_behind(): lax.ppermute(block, axis, [((i - distance) % count, i) for i in range(cou...  2.97 us
    ppermute x1, waiting for transfers between devices, from_behind(): lax.ppermute(block, axis, [((i - distance) % count, i) for i in range(cou...  1.2 us
    pallas_call x1, Pallas kernels, shards(): pl.pallas_call(functools.partial(collect, turns), out_shape=jax.ShapeDtyp...  1.06 us
    pallas_call x1, Pallas kernels, shards(): pl.pallas_call(functools.partial(last_step, turns), out_shape=jax.ShapeDt...  0.76 us
  transfers between devices with their start and end apart: 1, of which 1 were waited for; matrix products, arithmetic and copies ran while one was open for 0% of the time, Pallas kernels for 13%

profile of v5, /device:TPU:0, one launch (start us, length us, event | category | flops | bytes accessed | tf_op | source)
XLA Modules:
  0.0 29.3 jit_solution(16134166917111960329)
XLA Ops:
  0.0 3.0 %collective-permute-start = (bf16[192,512]{1,0:T(8,128)(2,1)}, bf16[192,512]{1,0:T(8,128)(2,1)S(1)}, u32[]{:S(2)}, u32[]{:S(2)}) collective-permute-start(bf16[192,512]{1,0:T(8,128)(2,1)} %occ_any.1), channel_id=1, source_target_pairs={{16,0},{0,16},{17,1},{1,17},{18,2},{2,18},{19,3},{3,19},{20,4},{4,... | collective-permute-start | bytes 589832 | tf_op jit(solution)/shard_map/ppermute | solution.py:33
  3.0 3.9 %shard_map.73 = (f32[32,64,128]{2,1,0:T(8,128)S(1)}, bf16[1,32,64,256]{3,2,1,0:T(8,128)(2,1)S(1)}, s32[32]{0:T(128)S(4)}, s32[16,128]{1,0:T(8,128)S(4)}) custom-call(s32[1]{0:T(128)} %bitcast.column_ref, s32[16,24]{1,0:T(8,128)} %list_any.1, s32[64]{0:T(128)} %slot_any.1, s32[1,2,24]{2,1,0:T(2,128)} %rows_any.1, s32[3,1,2,24]{3,2,1,0:T(2,128)} %pairs_any.1, ...), custom_call_target="tpu_custom_call" | custom-call | tf_op jit(solution)/shard_map/pallas_call | solution.py:295
  6.9 1.2 %collective-permute-done.occ_in = bf16[192,512]{1,0:T(8,128)(2,1)S(1)} collective-permute-done((bf16[192,512]{1,0:T(8,128)(2,1)}, bf16[192,512]{1,0:T(8,128)(2,1)S(1)}, u32[]{:S(2)}, u32[]{:S(2)}) %collective-permute-start) | collective-permute-done | bytes 196640 | tf_op jit(solution)/shard_map/ppermute | solution.py:33
  8.1 0.8 %shard_map.74 = s32[32,32,128]{2,1,0:T(8,128)S(1)} custom-call(s32[32]{0:T(128)S(4)} %get-tuple-element.10.occ_of_ref, bf16[32,64,256]{2,1,0:T(8,128)(2,1)S(1)} %bitcast.2, bf16[192,512]{1,0:T(8,128)(2,1)S(1)} %collective-permute-done.occ_in, f32[32,64,128]{2,1,0:T(8,128)S(1)} %get-tuple-element.12.before_ref), custom_call_target="tpu_custom_call" | custom-call | tf_op jit(solution)/shard_map/pallas_call | solution.py:334
  8.8 19.4 %all_to_all.5.received_ref = s32[32,32,128]{2,1,0:T(8,128)S(1)} all-to-all(s32[32,32,128]{2,1,0:T(8,128)S(1)} %shard_map.74), channel_id=1, replica_groups={{12,21,10,1,7,26,22,24,27,0,6,25,8,9,5,15,11,2,13,3,16,23,20,19,14,18,2..., dimensions={0} | all-to-all | bytes 1048576 | tf_op jit(solution)/shard_map/all_to_all | solution.py:340
  28.2 1.1 %shard_map.75 = bf16[8,32,512]{2,1,0:T(8,128)(2,1)} custom-call(s32[16,128]{1,0:T(8,128)S(4)} %get-tuple-element.9.target_ref, s32[32,32,128]{2,1,0:T(8,128)S(1)} %all_to_all.5.received_ref), custom_call_target="tpu_custom_call" | custom-call | tf_op jit(solution)/shard_map/pallas_call | solution.py:348
Async XLA Ops:
  0.0 8.1 %collective-permute-start = (bf16[192,512]{1,0:T(8,128)(2,1)}, bf16[192,512]{1,0:T(8,128)(2,1)S(1)}, u32[]{:S(2)}, u32[]{:S(2)}) collective-permute-start(bf16[192,512]{1,0:T(8,128)(2,1)} %occ_any.1), channel_id=1, source_target_pairs={{16,0},{0,16},{17,1},{1,17},{18,2},{2,18},{19,3},{3,19},{20,4},{4,... | collective-permute-start | bytes 589832 | tf_op jit(solution)/shard_map/ppermute | solution.py:33

commit v6 on v5

--- a/solution.py
+++ b/solution.py
@@ -203,11 +203,17 @@
     return jnp.concatenate([head, rounded(scaled[8:])], axis=0).astype(jnp.int32)
 
 
-def decoded(whole):
+def decoded(words):
     sub = lax.broadcasted_iota(jnp.int32, (8, OB), 0)
-    bits = jnp.sum(lax.shift_left(whole[:8] & 1, sub), axis=0, keepdims=True)
-    scale = jnp.exp2(bits.astype(jnp.float32) - BIAS) * (1.0 / LEVELS)
-    return whole.astype(jnp.float32) * scale
+    both = lax.shift_left(words[:8] & 0x10001, sub)
+    bits = jnp.sum(both, axis=0, keepdims=True)
+    scales = [
+        jnp.exp2(part.astype(jnp.float32) - BIAS)
+        for part in (bits & 0xFF, lax.shift_right_logical(bits, 16))
+    ]
+    low = lax.shift_left(words, 16).astype(jnp.float32) * (scales[0] * (2.0**-16 / LEVELS))
+    high = lax.shift_right_arithmetic(words, 16).astype(jnp.float32) * (scales[1] * (1.0 / LEVELS))
+    return low, high
 
 
 def rows_of(total, part, height):
@@ -256,8 +262,9 @@
         lows, highs = [], []
         for part in range(fit_count):
             words = received_ref[turns.index(part * ao_count + column)]
-            lows.append(decoded(lax.shift_right_arithmetic(lax.shift_left(words, 16), 16)))
-            highs.append(decoded(lax.shift_right_arithmetic(words, 16)))
+            low, high = decoded(words)
+            lows.append(low)
+            highs.append(high)
         for rank, parts in enumerate((lows, highs)):
             total = functools.reduce(jnp.add, parts)
             start = target_ref[column, rank] * height

time: 29.5 us -> 29.4 us (level)
  no operation moved by 1% of the time
where the time goes in v6:
time: 29.4 us; the launch traced here: 29.2 us
  blocking collectives  19.4 us (66%)
  Pallas kernels  5.62 us (19%)
  starting transfers between devices  2.97 us (10%)
  waiting for transfers between devices  1.2 us (4%)
    all_to_all x1, blocking collectives, shards(): lax.all_to_all(outgoing, ('fit', 'ao'), split_axis=0, concat_axis=0, tile...  19.4 us
    pallas_call x1, Pallas kernels, shards(): pl.pallas_call(first_step, out_shape=(total_shape, jax.ShapeDtypeStruct((...  3.9 us
    ppermute x1, starting transfers between devices, from_behind(): lax.ppermute(block, axis, [((i - distance) % count, i) for i in range(cou...  2.97 us
    ppermute x1, waiting for transfers between devices, from_behind(): lax.ppermute(block, axis, [((i - distance) % count, i) for i in range(cou...  1.2 us
    pallas_call x1, Pallas kernels, shards(): pl.pallas_call(functools.partial(collect, turns), out_shape=jax.ShapeDtyp...  0.98 us
    pallas_call x1, Pallas kernels, shards(): pl.pallas_call(functools.partial(last_step, turns), out_shape=jax.ShapeDt...  0.75 us
  transfers between devices with their start and end apart: 1, of which 1 were waited for; matrix products, arithmetic and copies ran while one was open for 0% of the time, Pallas kernels for 13%

profile of v6, /device:TPU:0, one launch (start us, length us, event | category | flops | bytes accessed | tf_op | source)
XLA Modules:
  0.0 29.2 jit_solution(17829167616549713578)
XLA Ops:
  0.0 3.0 %collective-permute-start = (bf16[192,512]{1,0:T(8,128)(2,1)}, bf16[192,512]{1,0:T(8,128)(2,1)S(1)}, u32[]{:S(2)}, u32[]{:S(2)}) collective-permute-start(bf16[192,512]{1,0:T(8,128)(2,1)} %occ_any.1), channel_id=1, source_target_pairs={{16,0},{0,16},{17,1},{1,17},{18,2},{2,18},{19,3},{3,19},{20,4},{4,... | collective-permute-start | bytes 589832 | tf_op jit(solution)/shard_map/ppermute | solution.py:33
  3.0 3.9 %shard_map.73 = (f32[32,64,128]{2,1,0:T(8,128)S(1)}, bf16[1,32,64,256]{3,2,1,0:T(8,128)(2,1)S(1)}, s32[32]{0:T(128)S(4)}, s32[16,128]{1,0:T(8,128)S(4)}) custom-call(s32[1]{0:T(128)} %bitcast.column_ref, s32[16,24]{1,0:T(8,128)} %list_any.1, s32[64]{0:T(128)} %slot_any.1, s32[1,2,24]{2,1,0:T(2,128)} %rows_any.1, s32[3,1,2,24]{3,2,1,0:T(2,128)} %pairs_any.1, ...), custom_call_target="tpu_custom_call" | custom-call | tf_op jit(solution)/shard_map/pallas_call | solution.py:302
  6.9 1.2 %collective-permute-done.occ_in = bf16[192,512]{1,0:T(8,128)(2,1)S(1)} collective-permute-done((bf16[192,512]{1,0:T(8,128)(2,1)}, bf16[192,512]{1,0:T(8,128)(2,1)S(1)}, u32[]{:S(2)}, u32[]{:S(2)}) %collective-permute-start) | collective-permute-done | bytes 196640 | tf_op jit(solution)/shard_map/ppermute | solution.py:33
  8.1 0.7 %shard_map.74 = s32[32,32,128]{2,1,0:T(8,128)S(1)} custom-call(s32[32]{0:T(128)S(4)} %get-tuple-element.10.occ_of_ref, bf16[32,64,256]{2,1,0:T(8,128)(2,1)S(1)} %bitcast.2, bf16[192,512]{1,0:T(8,128)(2,1)S(1)} %collective-permute-done.occ_in, f32[32,64,128]{2,1,0:T(8,128)S(1)} %get-tuple-element.12.before_ref), custom_call_target="tpu_custom_call" | custom-call | tf_op jit(solution)/shard_map/pallas_call | solution.py:341
  8.8 19.4 %all_to_all.5.received_ref = s32[32,32,128]{2,1,0:T(8,128)S(1)} all-to-all(s32[32,32,128]{2,1,0:T(8,128)S(1)} %shard_map.74), channel_id=1, replica_groups={{12,21,10,1,7,26,22,24,27,0,6,25,8,9,5,15,11,2,13,3,16,23,20,19,14,18,2..., dimensions={0} | all-to-all | bytes 1048576 | tf_op jit(solution)/shard_map/all_to_all | solution.py:347
  28.2 1.0 %shard_map.75 = bf16[8,32,512]{2,1,0:T(8,128)(2,1)} custom-call(s32[16,128]{1,0:T(8,128)S(4)} %get-tuple-element.9.target_ref, s32[32,32,128]{2,1,0:T(8,128)S(1)} %all_to_all.5.received_ref), custom_call_target="tpu_custom_call" | custom-call | tf_op jit(solution)/shard_map/pallas_call | solution.py:355
Async XLA Ops:
  0.0 8.1 %collective-permute-start = (bf16[192,512]{1,0:T(8,128)(2,1)}, bf16[192,512]{1,0:T(8,128)(2,1)S(1)}, u32[]{:S(2)}, u32[]{:S(2)}) collective-permute-start(bf16[192,512]{1,0:T(8,128)(2,1)} %occ_any.1), channel_id=1, source_target_pairs={{16,0},{0,16},{17,1},{1,17},{18,2},{2,18},{19,3},{3,19},{20,4},{4,... | collective-permute-start | bytes 589832 | tf_op jit(solution)/shard_map/ppermute | solution.py:33

commit v7 on v6

--- a/solution.py
+++ b/solution.py
@@ -19,7 +19,7 @@
 LIMIT = 48 * 1024 * 1024
 
 TURNS = (
-    12, 21, 10, 1, 7, 26, 22, 24, 27, 0, 6, 25, 8, 9, 5, 15, 11, 2, 13, 3, 16, 23, 20, 19,
+    20, 21, 10, 1, 7, 26, 22, 24, 27, 0, 6, 25, 8, 9, 5, 15, 11, 2, 13, 3, 16, 23, 12, 19,
     14, 18, 28, 17, 4, 29, 31, 30,
 )
 

time: 29.4 us -> 29.4 us (level)
  no operation moved by 1% of the time
where the time goes in v7:
time: 29.4 us; the launch traced here: 29.2 us
  blocking collectives  19.3 us (66%)
  Pallas kernels  5.64 us (19%)
  starting transfers between devices  2.97 us (10%)
  waiting for transfers between devices  1.2 us (4%)
    all_to_all x1, blocking collectives, shards(): lax.all_to_all(outgoing, ('fit', 'ao'), split_axis=0, concat_axis=0, tile...  19.3 us
    pallas_call x1, Pallas kernels, shards(): pl.pallas_call(first_step, out_shape=(total_shape, jax.ShapeDtypeStruct((...  3.9 us
    ppermute x1, starting transfers between devices, from_behind(): lax.ppermute(block, axis, [((i - distance) % count, i) for i in range(cou...  2.97 us
    ppermute x1, waiting for transfers between devices, from_behind(): lax.ppermute(block, axis, [((i - distance) % count, i) for i in range(cou...  1.2 us
    pallas_call x1, Pallas kernels, shards(): pl.pallas_call(functools.partial(collect, turns), out_shape=jax.ShapeDtyp...  0.98 us
    pallas_call x1, Pallas kernels, shards(): pl.pallas_call(functools.partial(last_step, turns), out_shape=jax.ShapeDt...  0.76 us
  transfers between devices with their start and end apart: 1, of which 1 were waited for; matrix products, arithmetic and copies ran while one was open for 0% of the time, Pallas kernels for 13%

profile of v7, /device:TPU:0, one launch (start us, length us, event | category | flops | bytes accessed | tf_op | source)
XLA Modules:
  0.0 29.2 jit_solution(16109655552882885919)
XLA Ops:
  0.0 3.0 %collective-permute-start = (bf16[192,512]{1,0:T(8,128)(2,1)}, bf16[192,512]{1,0:T(8,128)(2,1)S(1)}, u32[]{:S(2)}, u32[]{:S(2)}) collective-permute-start(bf16[192,512]{1,0:T(8,128)(2,1)} %occ_any.1), channel_id=1, source_target_pairs={{16,0},{0,16},{17,1},{1,17},{18,2},{2,18},{19,3},{3,19},{20,4},{4,... | collective-permute-start | bytes 589832 | tf_op jit(solution)/shard_map/ppermute | solution.py:33
  3.0 3.9 %shard_map.73 = (f32[32,64,128]{2,1,0:T(8,128)S(1)}, bf16[1,32,64,256]{3,2,1,0:T(8,128)(2,1)S(1)}, s32[32]{0:T(128)S(4)}, s32[16,128]{1,0:T(8,128)S(4)}) custom-call(s32[1]{0:T(128)} %bitcast.column_ref, s32[16,24]{1,0:T(8,128)} %list_any.1, s32[64]{0:T(128)} %slot_any.1, s32[1,2,24]{2,1,0:T(2,128)} %rows_any.1, s32[3,1,2,24]{3,2,1,0:T(2,128)} %pairs_any.1, ...), custom_call_target="tpu_custom_call" | custom-call | tf_op jit(solution)/shard_map/pallas_call | solution.py:302
  6.9 1.2 %collective-permute-done.occ_in = bf16[192,512]{1,0:T(8,128)(2,1)S(1)} collective-permute-done((bf16[192,512]{1,0:T(8,128)(2,1)}, bf16[192,512]{1,0:T(8,128)(2,1)S(1)}, u32[]{:S(2)}, u32[]{:S(2)}) %collective-permute-start) | collective-permute-done | bytes 196640 | tf_op jit(solution)/shard_map/ppermute | solution.py:33
  8.1 0.8 %shard_map.74 = s32[32,32,128]{2,1,0:T(8,128)S(1)} custom-call(s32[32]{0:T(128)S(4)} %get-tuple-element.10.occ_of_ref, bf16[32,64,256]{2,1,0:T(8,128)(2,1)S(1)} %bitcast.2, bf16[192,512]{1,0:T(8,128)(2,1)S(1)} %collective-permute-done.occ_in, f32[32,64,128]{2,1,0:T(8,128)S(1)} %get-tuple-element.12.before_ref), custom_call_target="tpu_custom_call" | custom-call | tf_op jit(solution)/shard_map/pallas_call | solution.py:341
  8.8 19.3 %all_to_all.5.received_ref = s32[32,32,128]{2,1,0:T(8,128)S(1)} all-to-all(s32[32,32,128]{2,1,0:T(8,128)S(1)} %shard_map.74), channel_id=1, replica_groups={{20,21,10,1,7,26,22,24,27,0,6,25,8,9,5,15,11,2,13,3,16,23,12,19,14,18,2..., dimensions={0} | all-to-all | bytes 1048576 | tf_op jit(solution)/shard_map/all_to_all | solution.py:347
  28.2 1.0 %shard_map.75 = bf16[8,32,512]{2,1,0:T(8,128)(2,1)} custom-call(s32[16,128]{1,0:T(8,128)S(4)} %get-tuple-element.9.target_ref, s32[32,32,128]{2,1,0:T(8,128)S(1)} %all_to_all.5.received_ref), custom_call_target="tpu_custom_call" | custom-call | tf_op jit(solution)/shard_map/pallas_call | solution.py:355
Async XLA Ops:
  0.0 8.1 %collective-permute-start = (bf16[192,512]{1,0:T(8,128)(2,1)}, bf16[192,512]{1,0:T(8,128)(2,1)S(1)}, u32[]{:S(2)}, u32[]{:S(2)}) collective-permute-start(bf16[192,512]{1,0:T(8,128)(2,1)} %occ_any.1), channel_id=1, source_target_pairs={{16,0},{0,16},{17,1},{1,17},{18,2},{2,18},{19,3},{3,19},{20,4},{4,... | collective-permute-start | bytes 589832 | tf_op jit(solution)/shard_map/ppermute | solution.py:33
